TPU v7x, 512 devices: a whole 4x4x16 slice. The times are simulated.
512 devices in a mesh: rep: 8 (over x, core), shard: 64 (over z, y).
Axes of the slice: x: 4, y: 4, z: 16, core: 2. Of those that a mesh axis runs over, the one named last changes fastest.
Arguments:
- grad_partial: bfloat16 [8, 192, 262144], P('rep', None, 'shard'), may hold values from -6 to 6
- block_order: int32 [192], replicated, may hold values from 0 to 191, each once
- owner_slot: int32 [192], replicated, may hold values from 0 to 63, as said below
- left_root: bfloat16 [8, 64, 512, 512], P('rep', 'shard'), may hold values from -1 to 4, as said below
- right_root: bfloat16 [8, 64, 512, 512], P('rep', 'shard'), may hold values from -1 to 4, as said below
Outputs:
- left_gram: float32 [8, 64, 512, 512], P('rep', 'shard')
- right_gram: float32 [8, 64, 512, 512], P('rep', 'shard')
- update: bfloat16 [192, 262144], P('rep', 'shard')
Inputs may be any that keep to these rules, and one draw needn't show every extreme that they name: `owner_slot`: entries g * 24 to (g + 1) * 24 - 1 are distinct for every group g. `left_root`: each matrix is symmetric. `right_root`: each matrix is symmetric.
All inputs are finite; a program needn't handle non-finite values.
Results may differ from a plain program's by a relative error of at most 0.02.
Values may be sent and summed in bfloat16 or wider, within the bound.
No kernel may reach another device: no remote copies, remote signals or barrier semaphores. Data moves between devices by JAX's collectives and lax.ppermute only.
A program may use at most 64 MiB of HBM per device.

v0:
```python
import jax
import jax.numpy as jnp
from jax import lax
from jax.sharding import PartitionSpec as P

graft_eps = 1e-06


def per_device(grad_partial, block_order, owner_slot, left_root, right_root):
    shard_count = lax.axis_size("shard")
    my_shard = lax.axis_index("shard")
    my_group = lax.axis_index("rep")
    slot_count = left_root.shape[1]
    block_size = left_root.shape[2]
    ordered = jnp.take(grad_partial[0], block_order, axis=0)
    summed = lax.psum_scatter(
        ordered.astype(jnp.float32).astype(jnp.bfloat16), "rep", scatter_dimension=0, tiled=True
    )
    group_size = summed.shape[0]
    flat_width = summed.shape[1]
    owners = lax.dynamic_slice_in_dim(owner_slot, my_group * group_size, group_size)
    targets = (
        jnp.arange(shard_count, dtype=jnp.int32)[:, None] * slot_count
        + jnp.arange(slot_count, dtype=jnp.int32)[None, :]
    )
    onehot = (owners[:, None, None] == targets[None]).astype(jnp.bfloat16)
    mine = lax.dynamic_index_in_dim(onehot, my_shard, 1, keepdims=False)
    received = jnp.einsum(
        "kif,ij->jkf",
        lax.all_gather(summed[None], "shard", axis=0, tiled=True),
        mine,
        preferred_element_type=jnp.float32,
    ).astype(jnp.bfloat16)
    blocks = received.reshape(slot_count, block_size, block_size)
    left_stat = (
        jnp.einsum("sab,scb->sac", blocks, blocks, preferred_element_type=jnp.float32) / block_size
    )
    right_stat = (
        jnp.einsum("sba,sbc->sac", blocks, blocks, preferred_element_type=jnp.float32) / block_size
    )
    half_product = jnp.einsum(
        "sab,sbc->sac", left_root[0], blocks, preferred_element_type=jnp.float32
    ).astype(jnp.bfloat16)
    shaped = jnp.einsum(
        "sab,sbc->sac", half_product, right_root[0], preferred_element_type=jnp.float32
    )
    plain = blocks.astype(jnp.float32)
    graft_ratio = jnp.sqrt(jnp.mean(plain * plain, axis=(1, 2)) + graft_eps) / jnp.sqrt(
        jnp.mean(shaped * shaped, axis=(1, 2)) + graft_eps
    )
    grafted = (shaped * graft_ratio[:, None, None]).astype(jnp.bfloat16)
    returned = lax.all_to_all(
        grafted.reshape(slot_count, shard_count, flat_width),
        "shard",
        split_axis=1,
        concat_axis=1,
        tiled=True,
    )
    update = jnp.einsum("jof,ioj->if", returned, onehot, preferred_element_type=jnp.float32).astype(
        jnp.bfloat16
    )
    return (left_stat[None], right_stat[None], update)


def solution(mesh):
    return jax.shard_map(
        per_device,
        mesh=mesh,
        in_specs=(
            P("rep", None, "shard"),
            P(),
            P(),
            P("rep", "shard", None, None),
            P("rep", "shard", None, None),
        ),
        out_specs=(P("rep", "shard", None, None), P("rep", "shard", None, None), P("rep", "shard")),
        check_vma=False,
    )
```

profile of v0, /device:TPU:4, one launch (start us, length us, event | category | flops | bytes accessed | tf_op | source)
XLA Modules:
  0.0 304.7 jit_solution(17521476056484081968)
XLA Ops:
  7.2 0.0 copy-start
  7.2 0.0 reduce-scatter.2.cloned.1.call-start
  7.2 0.8 compare_select_fusion
  8.0 0.7 compare_and_fusion
  8.7 0.0 copy-done
  8.7 1.5 gather_fusion
  10.3 1.4 broadcast_select_fusion
  11.6 0.0 copy-start.1
  11.6 0.0 reduce-scatter.2.cloned.1.call-update
  11.6 0.0 all-gather.3.cloned.1.call-start
  11.7 40.0 %reduce-scatter.2.cloned.1.call-done = bf16[24,4096]{1,0:T(8,128)(2,1)} async-done(((bf16[192,4096]{1,0:T(8,128)(2,1)}), bf16[24,4096]{1,0:T(8,128)(2,1)}) %reduce-scatter.2.cloned.1.call-update) | async-done | bytes 196624 | tf_op jit(solution)/shard_map/reduce_scatter | solution.py:16
  51.7 0.0 all-gather.3.cloned.1.call-update
  51.7 0.0 copy-done.1
  51.7 0.1 dynamic_slice.7
  51.8 177.7 %all-gather.3.cloned.1.call-done = bf16[1536,4096]{1,0:T(8,128)(2,1)} async-done(((bf16[24,4096]{1,0:T(8,128)(2,1)}), bf16[1536,4096]{1,0:T(8,128)(2,1)}) %all-gather.3.cloned.1.call-update) | async-done | bytes 12582928 | tf_op jit(solution)/shard_map/all_gather | solution.py:30
  229.5 7.3 %fusion.9 = bf16[1,64,4096]{2,0,1:T(2,128)(2,1)S(1)} fusion(bf16[64,24,4096]{2,1,0:T(8,128)(2,1)} %bitcast.37, s32[]{:T(128)S(6)} %select_n.17, s32[24]{0:T(128)S(1)} %dynamic_slice.7), kind=kOutput, calls=%fused_computation.21 | convolution fusion | flops 12582960 | bytes 13107300 | tf_op jit(solution)/shard_map/kif,ij->jkf/dot_general | solution.py:28
  236.8 1.2 multiply_reduce_fusion.1
  238.1 0.2 reshape.129
  238.3 2.8 multiply_reduce_fusion
  242.5 0.9 multiply_convert_fusion
  243.4 3.4 %reshape.146 = bf16[1,64,4096]{2,0,1:T(2,128)(2,1)S(1)} reshape(bf16[512,512]{1,0:T(8,128)(2,1)} %multiply_convert_fusion) | data formatting | bytes 1048576 | tf_op jit(solution)/shard_map/reshape | solution.py:53
  246.8 0.5 broadcast.57
  247.4 4.6 %reduce.6 = bf16[64,4096]{1,0:T(8,128)(2,1)} reduce(bf16[64,1,4096]{2,1,0:T(2,128)(2,1)S(1)} %bitcast.38, bf16[]{:T(256)} %broadcast.57), dimensions={1}, to_apply=%bitcast.23.reduce_sub_computation | reduce | bytes 1048578
  251.9 2.2 reshape.147
  254.1 9.3 %all-to-all-start = ((bf16[64,2,2048]{2,1,0:T(2,128)(2,1)}), bf16[64,2,2048]{2,1,0:T(2,128)(2,1)S(1)}, u32[]{:S(2)}, u32[]{:S(2)}) async-start(bf16[64,2,2048]{2,1,0:T(2,128)(2,1)} %reshape.147), calls=%async_computation.1 | async-start | bytes 1048576 | tf_op jit(solution)/shard_map/all_to_all | solution.py:52
  263.4 1.4 fusion.1
  264.9 1.4 fusion
  266.3 29.6 %all-to-all-done = bf16[64,2,2048]{2,1,0:T(2,128)(2,1)S(1)} async-done(((bf16[64,2,2048]{2,1,0:T(2,128)(2,1)}), bf16[64,2,2048]{2,1,0:T(2,128)(2,1)S(1)}, u32[]{:S(2)}, u32[]{:S(2)}) %all-to-all-start) | async-done | bytes 524320 | tf_op jit(solution)/shard_map/all_to_all | solution.py:52
  295.9 0.5 reshape.148
  296.5 1.3 convolution_convert_fusion
  (1 shorter events, 0.0 us)
Async XLA Ops:
  7.2 1.5 copy-start
  7.2 44.5 %reduce-scatter.2.cloned.1.call-start = ((), (), s32[]{:S(2)}) async-start(), calls=%async_computation.2 | async-start | bytes 1769472 | tf_op jit(solution)/shard_map/reduce_scatter | solution.py:16
  11.6 40.1 %copy-start.1 = (s32[192]{0:T(256)S(1)}, s32[192]{0:T(256)}, u32[]{:S(2)}) copy-start(s32[192]{0:T(256)} %param.7) | copy-start | bytes 2308
  11.6 217.9 %all-gather.3.cloned.1.call-start = ((), (), s32[]{:S(2)}) async-start(), calls=%async_computation.3 | async-start | bytes 12779520 | tf_op jit(solution)/shard_map/all_gather | solution.py:30
  254.1 41.8 %all-to-all-start = ((bf16[64,2,2048]{2,1,0:T(2,128)(2,1)}), bf16[64,2,2048]{2,1,0:T(2,128)(2,1)S(1)}, u32[]{:S(2)}, u32[]{:S(2)}) async-start(bf16[64,2,2048]{2,1,0:T(2,128)(2,1)} %reshape.147), calls=%async_computation.1 | async-start | bytes 1048576 | tf_op jit(solution)/shard_map/all_to_all | solution.py:52
Sparse Core Ops, SparseCore 0:
  11.8 39.8 reduce-scatter.1
  54.6 174.8 all-gather.2
where the time goes:
time: 305 us
  waiting for transfers between devices  247 us (81%)
  between operations  15.5 us (5%)
  matrix products  14.4 us (5%)
  other arithmetic  9.59 us (3%)
  starting transfers between devices  9.34 us (3%)
  local copies, waits for them, and re-layouts  8.49 us (3%)
    all_gather x1, waiting for transfers between devices, per_device(): lax.all_gather(summed[None], 'shard', axis=0, tiled=True)  178 us
    reduce_scatter x1, waiting for transfers between devices, per_device(): lax.psum_scatter(ordered.astype(jnp.float32).astype(jnp.bfloat16), 'rep',...  40 us
    all_to_all x1, waiting for transfers between devices, per_device(): lax.all_to_all(grafted.reshape(slot_count, shard_count, flat_width), 'sha...  29.6 us
    all_to_all x1, starting transfers between devices, per_device(): lax.all_to_all(grafted.reshape(slot_count, shard_count, flat_width), 'sha...  9.25 us
    dot_general x1, matrix products, per_device(): jnp.einsum('kif,ij->jkf', lax.all_gather(summed[None], 'shard', axis=0, t...  7.32 us
  transfers between devices with their start and end apart: 3, of which 3 were waited for; matrix products, arithmetic and copies ran while one was open for 1% of the time, Pallas kernels for 0%

commit v1 on v0

v1 whole, which is shorter than its diff:
```python
import jax
import jax.numpy as jnp
from jax import lax
from jax.sharding import Mesh, PartitionSpec as P

graft_eps = 1e-06
rows = 8


def swap_core(value):
    return lax.ppermute(value, "core", [(0, 1), (1, 0)])


def per_device(grad_partial, block_order, owner_slot, left_root, right_root):
    x_count = lax.axis_size("x")
    shard_count = lax.axis_size("z") * lax.axis_size("y")
    my_shard = lax.axis_index(("z", "y"))
    my_core = lax.axis_index("core")
    my_group = lax.axis_index(("x", "core"))
    block_size = left_root.shape[2]
    block_count = grad_partial.shape[1]
    group_size = block_count // (2 * x_count)
    by_core = block_order.reshape(x_count, 2, group_size)
    partial = grad_partial[0].reshape(block_count, rows, block_size)
    kept_order = lax.dynamic_index_in_dim(by_core, my_core, 1, keepdims=False).reshape(-1)
    sent_order = lax.dynamic_index_in_dim(by_core, 1 - my_core, 1, keepdims=False).reshape(-1)
    kept = jnp.take(partial, kept_order, axis=0, mode="clip")
    sent = jnp.take(partial, sent_order, axis=0, mode="clip")
    chip = (kept.astype(jnp.float32) + swap_core(sent).astype(jnp.float32)).astype(jnp.bfloat16)
    chips = lax.all_to_all(chip, "x", 0, 0, tiled=True).reshape(
        x_count, group_size, rows, block_size
    )
    summed = jnp.sum(chips.astype(jnp.float32), axis=0).astype(jnp.bfloat16)

    owners = lax.dynamic_slice_in_dim(owner_slot, my_group * group_size, group_size)
    held = jnp.zeros((shard_count,), jnp.int32).at[owners].set(
        jnp.arange(group_size, dtype=jnp.int32)
    )
    owns = jnp.any(owners == my_shard)
    outgoing = jnp.take(summed, held, axis=0, mode="clip")
    received = lax.all_to_all(outgoing, ("z", "y"), 0, 0, tiled=True)
    block = jnp.where(owns, received.reshape(block_size, block_size), 0).astype(jnp.bfloat16)

    left_stat = (
        jnp.einsum("ab,cb->ac", block, block, preferred_element_type=jnp.float32) / block_size
    )
    right_stat = (
        jnp.einsum("ba,bc->ac", block, block, preferred_element_type=jnp.float32) / block_size
    )
    half_product = jnp.dot(left_root[0, 0], block, preferred_element_type=jnp.float32).astype(
        jnp.bfloat16
    )
    shaped = jnp.dot(half_product, right_root[0, 0], preferred_element_type=jnp.float32)
    plain = block.astype(jnp.float32)
    graft_ratio = jnp.sqrt(jnp.mean(plain * plain) + graft_eps) / jnp.sqrt(
        jnp.mean(shaped * shaped) + graft_eps
    )
    grafted = (shaped * graft_ratio).astype(jnp.bfloat16)
    returned = lax.all_to_all(
        grafted.reshape(shard_count, rows, block_size), ("z", "y"), 0, 0, tiled=True
    )
    update = jnp.take(returned, owners, axis=0, mode="clip").reshape(group_size, rows * block_size)
    return (left_stat[None, None], right_stat[None, None], update)


def solution(mesh):
    rep_count, shard_count = mesh.devices.shape
    split = Mesh(
        mesh.devices.reshape(rep_count // 2, 2, shard_count // 4, 4), ("x", "core", "z", "y")
    )
    return jax.shard_map(
        per_device,
        mesh=split,
        in_specs=(
            P(("x", "core"), None, ("z", "y")),
            P(),
            P(),
            P(("x", "core"), ("z", "y"), None, None),
            P(("x", "core"), ("z", "y"), None, None),
        ),
        out_specs=(
            P(("x", "core"), ("z", "y"), None, None),
            P(("x", "core"), ("z", "y"), None, None),
            P(("x", "core"), ("z", "y")),
        ),
        check_vma=False,
    )
```

time: 305 us -> 125 us (0.41)
  the two profiles are of different devices: /device:TPU:4 before, /device:TPU:8 now
where the time goes in v1:
time: 125 us
  blocking collectives  50.4 us (40%)
  waiting for transfers between devices  41.9 us (34%)
  starting transfers between devices  12.2 us (10%)
  local copies, waits for them, and re-layouts  7.77 us (6%)
  other arithmetic  5.54 us (4%)
  matrix products  4.77 us (4%)
  between operations  2.13 us (2%)
    all_to_all x1, blocking collectives, per_device(): received = lax.all_to_all(outgoing, ('z', 'y'), 0, 0, tiled=True)  50.4 us
    all_to_all x1, waiting for transfers between devices, per_device(): lax.all_to_all(grafted.reshape(shard_count, rows, block_size), ('z', 'y')...  28.8 us
    all_to_all x1, waiting for transfers between devices, per_device(): lax.all_to_all(chip, 'x', 0, 0, tiled=True)  11.2 us
    all_to_all x1, starting transfers between devices, per_device(): lax.all_to_all(grafted.reshape(shard_count, rows, block_size), ('z', 'y')...  5.95 us
    all_to_all x1, starting transfers between devices, per_device(): lax.all_to_all(chip, 'x', 0, 0, tiled=True)  4.29 us
    unnamed x8, local copies, waits for them, and re-layouts  2.82 us
  transfers between devices with their start and end apart: 3, of which 3 were waited for; matrix products, arithmetic and copies ran while one was open for 4% of the time, Pallas kernels for 0%

profile of v1, /device:TPU:8, one launch (start us, length us, event | category | flops | bytes accessed | tf_op | source)
XLA Modules:
  0.0 124.6 jit_solution(255361833944114027)
XLA Ops:
  0.6 0.0 copy-start
  0.7 0.8 reshape.30
  1.5 0.1 reshape.44
  1.6 2.1 %copy.12 = bf16[24,8,8,512]{3,2,1,0:T(8,128)(2,1)S(1)} copy(bf16[24,8,8,512]{3,1,2,0:T(8,128)(2,1)} %bitcast.42) | data formatting | bytes 3145728
  3.7 1.5 %gather_fusion.1 = bf16[96,8,512]{2,1,0:T(8,128)(2,1)} fusion(bf16[192,8,512]{2,1,0:T(8,128)(2,1)S(1)} %bitcast.39, s32[1024]{0:T(1024)S(1)} %pad_clamp_fusion.2), kind=kCustom, calls=%fused_computation.1 | custom fusion | bytes 1573248 | tf_op jit(solution)/shard_map/jit(_take)/gather | solution.py:28
  5.2 1.9 %collective-permute-start = (bf16[96,8,512]{2,1,0:T(8,128)(2,1)}, bf16[96,8,512]{2,1,0:T(8,128)(2,1)}, u32[]{:S(2)}, u32[]{:S(2)}) collective-permute-start(bf16[96,8,512]{2,1,0:T(8,128)(2,1)} %gather_fusion.1), channel_id=1, source_target_pairs={{0,64},{64,0},{1,65},{65,1},{2,66},{66,2},{3,67},{67,3},{4,68},{68... | collective-permute-start | bytes 2359304 | tf_op jit(solution)/shard_map/ppermute | solution.py:11
  7.1 0.1 reshape.36
  7.2 0.6 gather_fusion
  7.8 0.0 copy-start.1
  7.8 1.9 %collective-permute-done = bf16[96,8,512]{2,1,0:T(8,128)(2,1)} collective-permute-done((bf16[96,8,512]{2,1,0:T(8,128)(2,1)}, bf16[96,8,512]{2,1,0:T(8,128)(2,1)}, u32[]{:S(2)}, u32[]{:S(2)}) %collective-permute-start) | collective-permute-done | bytes 786464 | tf_op jit(solution)/shard_map/ppermute | solution.py:11
  9.7 2.2 %add_convert_fusion = bf16[96,8,512]{2,1,0:T(8,128)(2,1)} fusion(bf16[96,8,512]{2,1,0:T(8,128)(2,1)} %collective-permute-done, bf16[96,8,512]{2,1,0:T(8,128)(2,1)S(1)} %gather_fusion), kind=kLoop, calls=%fused_computation.5 | loop fusion | flops 1572864 | bytes 2359296 | tf_op jit(solution)/shard_map/convert_element_type | solution.py:29
  11.9 4.3 %all-to-all-start = ((bf16[96,8,512]{2,1,0:T(8,128)(2,1)}), bf16[96,8,512]{2,1,0:T(8,128)(2,1)S(1)}, u32[]{:S(2)}, u32[]{:S(2)}) async-start(bf16[96,8,512]{2,1,0:T(8,128)(2,1)} %add_convert_fusion), calls=%async_computation | async-start | bytes 1572864 | tf_op jit(solution)/shard_map/all_to_all | solution.py:30
  16.2 0.0 copy-done.1
  16.2 0.7 compare_reduce_fusion
  16.9 0.6 scatter_custom_fusion
  17.6 11.2 %all-to-all-done = bf16[96,8,512]{2,1,0:T(8,128)(2,1)S(1)} async-done(((bf16[96,8,512]{2,1,0:T(8,128)(2,1)}), bf16[96,8,512]{2,1,0:T(8,128)(2,1)S(1)}, u32[]{:S(2)}, u32[]{:S(2)}) %all-to-all-start) | async-done | bytes 786464 | tf_op jit(solution)/shard_map/all_to_all | solution.py:30
  28.8 0.1 reduce_sum.30
  28.9 0.0 copy-start.2
  28.9 0.6 gather_fusion.2
  29.5 50.4 %all_to_all.15 = bf16[64,8,512]{2,1,0:T(8,128)(2,1)S(1)} all-to-all(bf16[64,8,512]{2,1,0:T(8,128)(2,1)S(1)} %gather_fusion.2), channel_id=1, replica_groups=mesh['x'=4,'core'=2,'z'=16,'y'=4] {'z','y'}, dimensions={0} | all-to-all | bytes 1048576 | tf_op jit(solution)/shard_map/all_to_all | solution.py:41
  79.9 1.5 %multiply_reduce_fusion.1 = (f32[]{:T(128)}, bf16[64,8,512]{2,0,1:T(8,128)(2,1)S(1)}) fusion(bf16[64,8,512]{2,1,0:T(8,128)(2,1)S(1)} %all_to_all.15, pred[]{:T(512)} %get-tuple-element.7), kind=kLoop, calls=%fused_computation.15 | loop fusion | flops 1048575 | bytes 1048581 | tf_op jit(solution)/shard_map/reduce_sum | solution.py:55
  81.5 0.0 copy-done
  81.5 0.0 copy-done.2
  81.5 1.7 %multiply_reduce_fusion = (f32[]{:T(128)}, f32[512,512]{1,0:T(8,128)S(1)}) fusion(bf16[1,1,512,512]{3,2,1,0:T(8,128)(2,1)S(1)} %copy-done, bf16[1,1,512,512]{3,2,1,0:T(8,128)(2,1)S(1)} %copy-done.2, bf16[64,8,512]{2,0,1:T(8,128)(2,1)S(1)} %get-tuple-element.6), kind=kOutput, calls=%fused_computation.14 | convolution fusion | flops 537657344 | bytes 2621444 | tf_op jit(solution)/shard_map/dot_general | solution.py:53
  84.5 0.9 fusion.4
  85.4 6.0 %all-to-all-start.2 = ((bf16[64,8,512]{2,1,0:T(8,128)(2,1)}), bf16[64,8,512]{2,1,0:T(8,128)(2,1)S(1)}, u32[]{:S(2)}, u32[]{:S(2)}) async-start(bf16[64,8,512]{2,1,0:T(8,128)(2,1)} %fusion.4), calls=%async_computation.2 | async-start | bytes 1048576 | tf_op jit(solution)/shard_map/all_to_all | solution.py:59
  91.4 1.7 %fusion.2 = f32[1,1,512,512]{3,2,1,0:T(8,128)} fusion(bf16[64,8,512]{2,0,1:T(8,128)(2,1)S(1)} %get-tuple-element.6), kind=kOutput, calls=%fused_computation.10 | convolution fusion | flops 268697600 | bytes 1572864 | tf_op jit(solution)/shard_map/ab,cb->ac/dot_general | solution.py:45
  93.1 1.4 %fusion.1 = f32[1,1,512,512]{3,2,1,0:T(8,128)} fusion(bf16[64,8,512]{2,0,1:T(8,128)(2,1)S(1)} %get-tuple-element.6), kind=kOutput, calls=%fused_computation.8 | convolution fusion | flops 268697600 | bytes 1572864 | tf_op jit(solution)/shard_map/ba,bc->ac/dot_general | solution.py:48
  94.5 28.8 %all-to-all-done.2 = bf16[64,8,512]{2,1,0:T(8,128)(2,1)S(1)} async-done(((bf16[64,8,512]{2,1,0:T(8,128)(2,1)}), bf16[64,8,512]{2,1,0:T(8,128)(2,1)S(1)}, u32[]{:S(2)}, u32[]{:S(2)}) %all-to-all-start.2) | async-done | bytes 524320 | tf_op jit(solution)/shard_map/all_to_all | solution.py:59
  123.3 0.6 gather_fusion.3
  123.9 0.7 copy.13
  (7 shorter events, 0.1 us)
Async XLA Ops:
  0.6 80.8 %copy-start = (bf16[1,1,512,512]{3,2,1,0:T(8,128)(2,1)S(1)}, bf16[1,1,512,512]{3,2,1,0:T(8,128)(2,1)}, u32[]{:S(2)}) copy-start(bf16[1,1,512,512]{3,2,1,0:T(8,128)(2,1)} %param.9) | copy-start | bytes 1572868
  5.2 4.5 %collective-permute-start = (bf16[96,8,512]{2,1,0:T(8,128)(2,1)}, bf16[96,8,512]{2,1,0:T(8,128)(2,1)}, u32[]{:S(2)}, u32[]{:S(2)}) collective-permute-start(bf16[96,8,512]{2,1,0:T(8,128)(2,1)} %gather_fusion.1), channel_id=1, source_target_pairs={{0,64},{64,0},{1,65},{65,1},{2,66},{66,2},{3,67},{67,3},{4,68},{68... | collective-permute-start | bytes 2359304 | tf_op jit(solution)/shard_map/ppermute | solution.py:11
  7.8 8.4 %copy-start.1 = (s32[192]{0:T(256)S(1)}, s32[192]{0:T(256)}, u32[]{:S(2)}) copy-start(s32[192]{0:T(256)} %param.7) | copy-start | bytes 2308
  11.9 16.9 %all-to-all-start = ((bf16[96,8,512]{2,1,0:T(8,128)(2,1)}), bf16[96,8,512]{2,1,0:T(8,128)(2,1)S(1)}, u32[]{:S(2)}, u32[]{:S(2)}) async-start(bf16[96,8,512]{2,1,0:T(8,128)(2,1)} %add_convert_fusion), calls=%async_computation | async-start | bytes 1572864 | tf_op jit(solution)/shard_map/all_to_all | solution.py:30
  28.9 52.5 %copy-start.2 = (bf16[1,1,512,512]{3,2,1,0:T(8,128)(2,1)S(1)}, bf16[1,1,512,512]{3,2,1,0:T(8,128)(2,1)}, u32[]{:S(2)}) copy-start(bf16[1,1,512,512]{3,2,1,0:T(8,128)(2,1)} %param.8) | copy-start | bytes 1572868
  85.4 37.9 %all-to-all-start.2 = ((bf16[64,8,512]{2,1,0:T(8,128)(2,1)}), bf16[64,8,512]{2,1,0:T(8,128)(2,1)S(1)}, u32[]{:S(2)}, u32[]{:S(2)}) async-start(bf16[64,8,512]{2,1,0:T(8,128)(2,1)} %fusion.4), calls=%async_computation.2 | async-start | bytes 1048576 | tf_op jit(solution)/shard_map/all_to_all | solution.py:59

commit v2 on v1

v2 whole, which is shorter than its diff:
```python
import jax
import jax.numpy as jnp
from jax import lax
from jax.experimental import pallas as pl
from jax.experimental.pallas import tpu as pltpu
from jax.sharding import Mesh, PartitionSpec as P

graft_eps = 1e-06
rows = 8


def swap_core(value):
    return lax.ppermute(value, "core", [(0, 1), (1, 0)])


def place_kernel(core, order, partial, sent_out, kept_out):
    group_size = order.shape[0] // 8
    for chip in range(4):
        for i in range(group_size):
            place = chip * group_size + i
            sent_out[place] = partial[order[(2 * chip + 1 - core[0]) * group_size + i]]
            kept_out[place] = partial[order[(2 * chip + core[0]) * group_size + i]]


def place(core, order, partial):
    smem = pl.BlockSpec(memory_space=pltpu.SMEM)
    vmem = pl.BlockSpec(memory_space=pltpu.VMEM)
    half = jax.ShapeDtypeStruct((partial.shape[0] // 2,) + partial.shape[1:], partial.dtype)
    return pl.pallas_call(
        place_kernel,
        out_shape=(half, half),
        in_specs=[smem, smem, vmem],
        out_specs=(vmem, vmem),
        compiler_params=pltpu.CompilerParams(vmem_limit_bytes=32 * 1024 * 1024),
        cost_estimate=pl.CostEstimate(
            flops=partial.size, bytes_accessed=4 * partial.size, transcendentals=0
        ),
    )(core, order, partial)


def slots_kernel(held, chips, outgoing, summed):
    for i in range(summed.shape[0]):
        total = chips[0, i].astype(jnp.float32)
        for x in range(1, chips.shape[0]):
            total += chips[x, i].astype(jnp.float32)
        summed[i] = total.astype(summed.dtype)
    for j in range(outgoing.shape[0]):
        outgoing[j] = summed[held[j]]


def slots(held, chips):
    vmem = pl.BlockSpec(memory_space=pltpu.VMEM)
    return pl.pallas_call(
        slots_kernel,
        out_shape=jax.ShapeDtypeStruct((held.shape[0],) + chips.shape[2:], chips.dtype),
        in_specs=[pl.BlockSpec(memory_space=pltpu.SMEM), vmem],
        out_specs=vmem,
        scratch_shapes=[pltpu.VMEM(chips.shape[1:], chips.dtype)],
        compiler_params=pltpu.CompilerParams(vmem_limit_bytes=32 * 1024 * 1024),
        cost_estimate=pl.CostEstimate(
            flops=chips.size, bytes_accessed=4 * chips.size, transcendentals=0
        ),
    )(held, chips)


def middle_kernel(owns, received, left, right, block_out, grafted_out):
    size = left.shape[0]
    block = jnp.where(owns[0] > 0, received[...].astype(jnp.float32), 0.0)
    plain = block.astype(jnp.bfloat16)
    block_out[...] = plain
    half = jnp.dot(left[...], plain, preferred_element_type=jnp.float32).astype(jnp.bfloat16)
    shaped = jnp.dot(half, right[...], preferred_element_type=jnp.float32)
    scale = 1.0 / (size * size)
    ratio = jnp.sqrt(jnp.sum(block * block, keepdims=True) * scale + graft_eps) / jnp.sqrt(
        jnp.sum(shaped * shaped, keepdims=True) * scale + graft_eps
    )
    grafted_out[...] = (shaped * ratio).astype(jnp.bfloat16)


def middle(owns, received, left, right):
    size = left.shape[0]
    vmem = pl.BlockSpec(memory_space=pltpu.VMEM)
    return pl.pallas_call(
        middle_kernel,
        out_shape=(jax.ShapeDtypeStruct((size, size), jnp.bfloat16),) * 2,
        in_specs=[pl.BlockSpec(memory_space=pltpu.SMEM)] + [vmem] * 3,
        out_specs=(vmem, vmem),
        compiler_params=pltpu.CompilerParams(vmem_limit_bytes=32 * 1024 * 1024),
        cost_estimate=pl.CostEstimate(
            flops=4 * size * size * size, bytes_accessed=10 * size * size, transcendentals=2
        ),
    )(owns, received, left, right)


def per_device(grad_partial, block_order, owner_slot, left_root, right_root):
    shard_count = lax.axis_size("z") * lax.axis_size("y")
    my_core = lax.axis_index("core")
    my_shard = lax.axis_index(("z", "y"))
    my_group = lax.axis_index(("x", "core"))
    block_size = left_root.shape[2]
    block_count = grad_partial.shape[1]
    group_size = block_count // (2 * lax.axis_size("x"))

    partial = grad_partial[0].reshape(block_count, rows, block_size)
    sent, kept = place(my_core[None].astype(jnp.int32), block_order, partial)
    chip = kept + swap_core(sent)
    chips = lax.all_to_all(chip, "x", 0, 0, tiled=True)
    chips = chips.reshape(-1, group_size, rows, block_size)

    owners = lax.dynamic_slice_in_dim(owner_slot, my_group * group_size, group_size)
    held = jnp.zeros((shard_count,), jnp.int32).at[owners].set(
        jnp.arange(group_size, dtype=jnp.int32)
    )
    owns = jnp.any(owners == my_shard).astype(jnp.int32)[None]
    outgoing = slots(held, chips)
    received = lax.all_to_all(outgoing, ("z", "y"), 0, 0, tiled=True)
    block, grafted = middle(
        owns, received.reshape(block_size, block_size), left_root[0, 0], right_root[0, 0]
    )
    returned = lax.all_to_all(
        grafted.reshape(shard_count, rows, block_size), ("z", "y"), 0, 0, tiled=True
    )
    update = jnp.take(returned, owners, axis=0, mode="clip").reshape(group_size, rows * block_size)
    left_stat = jnp.einsum("ab,cb->ac", block, block, preferred_element_type=jnp.float32)
    right_stat = jnp.einsum("ba,bc->ac", block, block, preferred_element_type=jnp.float32)
    return (left_stat[None, None] / block_size, right_stat[None, None] / block_size, update)


def solution(mesh):
    rep_count, shard_count = mesh.devices.shape
    split = Mesh(
        mesh.devices.reshape(rep_count // 2, 2, shard_count // 4, 4), ("x", "core", "z", "y")
    )
    return jax.shard_map(
        per_device,
        mesh=split,
        in_specs=(
            P(("x", "core"), None, ("z", "y")),
            P(),
            P(),
            P(("x", "core"), ("z", "y"), None, None),
            P(("x", "core"), ("z", "y"), None, None),
        ),
        out_specs=(
            P(("x", "core"), ("z", "y"), None, None),
            P(("x", "core"), ("z", "y"), None, None),
            P(("x", "core"), ("z", "y")),
        ),
        check_vma=False,
    )
```

time: 125 us -> 119 us (0.952)
  blocking collectives: 50.4 us -> 0 us
  waiting for transfers between devices: 41.9 us -> 73.7 us
  starting transfers between devices: 12.2 us -> 30.9 us
  Pallas kernels: 0 us -> 4.18 us
  local copies, waits for them, and re-layouts: 7.77 us -> 4.02 us
  other arithmetic: 5.54 us -> 1.81 us
  matrix products: 4.77 us -> 2.89 us
    all_to_all x1 -> x0, blocking collectives: 50.4 us -> none  [per_device(): received = lax.all_to_all(outgoing, ('z', 'y'), 0, 0, tiled=True)]
    all_to_all x1 -> x2, waiting for transfers between devices: 11.2 us -> 42.4 us  [the longest x1 30.6 us: per_device(): received = lax.all_to_all(outgoing, ('z', 'y'), 0, 0, tiled=True)]
    all_to_all x1 -> x2, starting transfers between devices: 4.29 us -> 23 us  [the longest x1 18.7 us: per_device(): received = lax.all_to_all(outgoing, ('z', 'y'), 0, 0, tiled=True)]
    pallas_call x0 -> x3, Pallas kernels: none -> 4.18 us  [the longest x1 1.94 us: middle(): pl.pallas_call(middle_kernel, out_shape=(jax.ShapeDtypeStruct((size, size...]
    gather x3 -> x0, local copies, waits for them, and re-layouts: 2.73 us -> none  [the longest x1 1.52 us: per_device(): sent = jnp.take(partial, sent_order, axis=0, mode='clip')]
    convert_element_type x1 -> x0, other arithmetic: 2.22 us -> none  [per_device(): (kept.astype(jnp.float32) + swap_core(sent).astype(jnp.float32)).astype(j...]
    reduce_sum x2 -> x0, other arithmetic: 1.68 us -> none  [the longest x1 1.54 us: per_device(): jnp.mean(plain * plain) + graft_eps]
    dot_general x1 -> x0, matrix products: 1.66 us -> none  [per_device(): jnp.dot(half_product, right_root[0, 0], preferred_element_type=jnp.float32)]
  transfers between devices with their start and end apart: 3 -> 4, of which waited for: 3 -> 4; matrix products, arithmetic and copies ran while one was open for 4% -> 4% of each run, Pallas kernels for 0% -> 0%
where the time goes in v2:
time: 119 us
  waiting for transfers between devices  73.7 us (62%)
  starting transfers between devices  30.9 us (26%)
  Pallas kernels  4.18 us (4%)
  local copies, waits for them, and re-layouts  4.02 us (3%)
  matrix products  2.89 us (2%)
  other arithmetic  1.81 us (2%)
  between operations  1.38 us (1%)
    all_to_all x1, waiting for transfers between devices, per_device(): received = lax.all_to_all(outgoing, ('z', 'y'), 0, 0, tiled=True)  30.6 us
    all_to_all x1, waiting for transfers between devices, per_device(): lax.all_to_all(grafted.reshape(shard_count, rows, block_size), ('z', 'y')...  29 us
    all_to_all x1, starting transfers between devices, per_device(): received = lax.all_to_all(outgoing, ('z', 'y'), 0, 0, tiled=True)  18.7 us
    all_to_all x1, waiting for transfers between devices, per_device(): chips = lax.all_to_all(chip, 'x', 0, 0, tiled=True)  11.8 us
    all_to_all x1, starting transfers between devices, per_device(): lax.all_to_all(grafted.reshape(shard_count, rows, block_size), ('z', 'y')...  5.95 us
    all_to_all x1, starting transfers between devices, per_device(): chips = lax.all_to_all(chip, 'x', 0, 0, tiled=True)  4.29 us
    unnamed x10, local copies, waits for them, and re-layouts  2.81 us
  transfers between devices with their start and end apart: 4, of which 4 were waited for; matrix products, arithmetic and copies ran while one was open for 4% of the time, Pallas kernels for 0%

profile of v2, /device:TPU:8, one launch (start us, length us, event | category | flops | bytes accessed | tf_op | source)
XLA Modules:
  0.0 118.9 jit_solution(18094586260834331162)
XLA Ops:
  0.6 0.0 copy-start
  0.6 2.1 %copy.8 = bf16[24,8,8,512]{3,2,1,0:T(8,128)(2,1)S(1)} copy(bf16[24,8,8,512]{3,1,2,0:T(8,128)(2,1)} %bitcast.25) | data formatting | bytes 3145728
  2.7 0.0 copy-done
  2.7 0.8 shard_map.76
  3.5 1.9 %collective-permute-start = (bf16[96,8,512]{2,1,0:T(8,128)(2,1)S(1)}, bf16[96,8,512]{2,1,0:T(8,128)(2,1)S(1)}, u32[]{:S(2)}, u32[]{:S(2)}) collective-permute-start(bf16[96,8,512]{2,1,0:T(8,128)(2,1)S(1)} %get-tuple-element.8), channel_id=1, source_target_pairs={{0,64},{64,0},{1,65},{65,1},{2,66},{66,2},{3,67},{67,3},{4,68},{68... | collective-permute-start | bytes 2359304 | tf_op jit(solution)/shard_map/ppermute | solution.py:13
  5.4 2.3 %collective-permute-done = bf16[96,8,512]{2,1,0:T(8,128)(2,1)S(1)} collective-permute-done((bf16[96,8,512]{2,1,0:T(8,128)(2,1)S(1)}, bf16[96,8,512]{2,1,0:T(8,128)(2,1)S(1)}, u32[]{:S(2)}, u32[]{:S(2)}) %collective-permute-start) | collective-permute-done | bytes 786464 | tf_op jit(solution)/shard_map/ppermute | solution.py:13
  7.7 0.0 copy-start.3
  7.7 1.1 add.19
  8.7 4.3 %all-to-all-start = ((bf16[96,8,512]{2,1,0:T(8,128)(2,1)}), bf16[96,8,512]{2,1,0:T(8,128)(2,1)S(1)}, u32[]{:S(2)}, u32[]{:S(2)}) async-start(bf16[96,8,512]{2,1,0:T(8,128)(2,1)} %add.19), calls=%async_computation | async-start | bytes 1572864 | tf_op jit(solution)/shard_map/all_to_all | solution.py:107
  13.0 0.0 copy-start.1
  13.0 0.0 copy-start.2
  13.0 0.0 copy-done.3
  13.1 0.1 compare_select_fusion
  13.1 0.6 scatter_custom_fusion.held
  13.8 11.8 %all-to-all-done = bf16[96,8,512]{2,1,0:T(8,128)(2,1)S(1)} async-done(((bf16[96,8,512]{2,1,0:T(8,128)(2,1)}), bf16[96,8,512]{2,1,0:T(8,128)(2,1)S(1)}, u32[]{:S(2)}, u32[]{:S(2)}) %all-to-all-start) | async-done | bytes 786464 | tf_op jit(solution)/shard_map/all_to_all | solution.py:107
  25.6 1.5 %shard_map.77 = bf16[64,8,512]{2,1,0:T(8,128)(2,1)} custom-call(s32[64]{0:T(128)S(1)} %scatter_custom_fusion.held, bf16[4,24,8,512]{3,2,1,0:T(8,128)(2,1)S(1)} %bitcast.21), custom_call_target="tpu_custom_call" | custom-call | flops 393216 | bytes 1572864 | tf_op jit(solution)/shard_map/pallas_call | solution.py:53
  27.1 18.7 %all-to-all-start.1 = ((bf16[64,8,512]{2,1,0:T(8,128)(2,1)}), bf16[64,8,512]{2,1,0:T(8,128)(2,1)S(1)}, u32[]{:S(2)}, u32[]{:S(2)}) async-start(bf16[64,8,512]{2,1,0:T(8,128)(2,1)} %shard_map.77), calls=%async_computation.1 | async-start | bytes 1048576 | tf_op jit(solution)/shard_map/all_to_all | solution.py:116
  45.8 0.6 compare_reduce_fusion
  47.1 30.6 %all-to-all-done.1 = bf16[64,8,512]{2,1,0:T(8,128)(2,1)S(1)} async-done(((bf16[64,8,512]{2,1,0:T(8,128)(2,1)}), bf16[64,8,512]{2,1,0:T(8,128)(2,1)S(1)}, u32[]{:S(2)}, u32[]{:S(2)}) %all-to-all-start.1) | async-done | bytes 524320 | tf_op jit(solution)/shard_map/all_to_all | solution.py:116
  77.7 0.0 copy-done.1
  77.7 0.0 copy-done.2
  77.7 1.9 %shard_map.78 = (bf16[512,512]{1,0:T(8,128)(2,1)S(1)}, bf16[512,512]{1,0:T(8,128)(2,1)}) custom-call(s32[1]{0:T(128)} %bitcast.owns, bf16[512,512]{1,0:T(8,128)(2,1)S(1)} %bitcast.22, bf16[512,512]{1,0:T(8,128)(2,1)S(1)} %bitcast.23, bf16[512,512]{1,0:T(8,128)(2,1)S(1)} %bitcast.24), custom_call_target="tpu_custom_call" | custom-call | flops 536870912 | bytes 2621440 | tf_op jit(solution)/shard_map/pallas_call | solution.py:83
  79.6 6.0 %all-to-all-start.2 = ((bf16[64,8,512]{2,1,0:T(8,128)(2,1)}), bf16[64,8,512]{2,1,0:T(8,128)(2,1)S(1)}, u32[]{:S(2)}, u32[]{:S(2)}) async-start(bf16[64,8,512]{2,1,0:T(8,128)(2,1)} %bitcast.8), calls=%async_computation.2 | async-start | bytes 1048576 | tf_op jit(solution)/shard_map/all_to_all | solution.py:120
  85.6 1.4 %fusion.1 = f32[1,1,512,512]{3,2,1,0:T(8,128)} fusion(bf16[512,512]{1,0:T(8,128)(2,1)S(1)} %get-tuple-element.9), kind=kOutput, calls=%fused_computation.5 | convolution fusion | flops 268697600 | bytes 1572864 | tf_op jit(solution)/shard_map/ab,cb->ac/dot_general | solution.py:124
  87.1 1.4 %fusion = f32[1,1,512,512]{3,2,1,0:T(8,128)} fusion(bf16[512,512]{1,0:T(8,128)(2,1)S(1)} %get-tuple-element.9), kind=kOutput, calls=%fused_computation.3 | convolution fusion | flops 268697600 | bytes 1572864 | tf_op jit(solution)/shard_map/ba,bc->ac/dot_general | solution.py:125
  88.5 29.0 %all-to-all-done.2 = bf16[64,8,512]{2,1,0:T(8,128)(2,1)S(1)} async-done(((bf16[64,8,512]{2,1,0:T(8,128)(2,1)}), bf16[64,8,512]{2,1,0:T(8,128)(2,1)S(1)}, u32[]{:S(2)}, u32[]{:S(2)}) %all-to-all-start.2) | async-done | bytes 524320 | tf_op jit(solution)/shard_map/all_to_all | solution.py:120
  117.5 0.6 gather_fusion
  118.1 0.7 copy.9
  (2 shorter events, 0.0 us)
Async XLA Ops:
  0.6 2.1 %copy-start = (s32[192]{0:T(256)S(1)}, s32[192]{0:T(256)}, u32[]{:S(2)}) copy-start(s32[192]{0:T(256)} %order.1) | copy-start | bytes 2308
  3.5 4.2 %collective-permute-start = (bf16[96,8,512]{2,1,0:T(8,128)(2,1)S(1)}, bf16[96,8,512]{2,1,0:T(8,128)(2,1)S(1)}, u32[]{:S(2)}, u32[]{:S(2)}) collective-permute-start(bf16[96,8,512]{2,1,0:T(8,128)(2,1)S(1)} %get-tuple-element.8), channel_id=1, source_target_pairs={{0,64},{64,0},{1,65},{65,1},{2,66},{66,2},{3,67},{67,3},{4,68},{68... | collective-permute-start | bytes 2359304 | tf_op jit(solution)/shard_map/ppermute | solution.py:13
  7.7 5.4 %copy-start.3 = (s32[192]{0:T(256)S(1)}, s32[192]{0:T(256)}, u32[]{:S(2)}) copy-start(s32[192]{0:T(256)} %param.7) | copy-start | bytes 2308
  8.7 16.9 %all-to-all-start = ((bf16[96,8,512]{2,1,0:T(8,128)(2,1)}), bf16[96,8,512]{2,1,0:T(8,128)(2,1)S(1)}, u32[]{:S(2)}, u32[]{:S(2)}) async-start(bf16[96,8,512]{2,1,0:T(8,128)(2,1)} %add.19), calls=%async_computation | async-start | bytes 1572864 | tf_op jit(solution)/shard_map/all_to_all | solution.py:107
  13.0 64.7 %copy-start.1 = (bf16[1,1,512,512]{3,2,1,0:T(8,128)(2,1)S(1)}, bf16[1,1,512,512]{3,2,1,0:T(8,128)(2,1)}, u32[]{:S(2)}) copy-start(bf16[1,1,512,512]{3,2,1,0:T(8,128)(2,1)} %param.8) | copy-start | bytes 1572868
  13.0 64.7 %copy-start.2 = (bf16[1,1,512,512]{3,2,1,0:T(8,128)(2,1)S(1)}, bf16[1,1,512,512]{3,2,1,0:T(8,128)(2,1)}, u32[]{:S(2)}) copy-start(bf16[1,1,512,512]{3,2,1,0:T(8,128)(2,1)} %param.9) | copy-start | bytes 1572868
  27.1 50.6 %all-to-all-start.1 = ((bf16[64,8,512]{2,1,0:T(8,128)(2,1)}), bf16[64,8,512]{2,1,0:T(8,128)(2,1)S(1)}, u32[]{:S(2)}, u32[]{:S(2)}) async-start(bf16[64,8,512]{2,1,0:T(8,128)(2,1)} %shard_map.77), calls=%async_computation.1 | async-start | bytes 1048576 | tf_op jit(solution)/shard_map/all_to_all | solution.py:116
  79.6 37.9 %all-to-all-start.2 = ((bf16[64,8,512]{2,1,0:T(8,128)(2,1)}), bf16[64,8,512]{2,1,0:T(8,128)(2,1)S(1)}, u32[]{:S(2)}, u32[]{:S(2)}) async-start(bf16[64,8,512]{2,1,0:T(8,128)(2,1)} %bitcast.8), calls=%async_computation.2 | async-start | bytes 1048576 | tf_op jit(solution)/shard_map/all_to_all | solution.py:120

commit v3 on v2

v3 whole, which is shorter than its diff:
```python
import jax
import jax.numpy as jnp
from jax import lax
from jax.experimental import pallas as pl
from jax.experimental.pallas import tpu as pltpu
from jax.sharding import Mesh, PartitionSpec as P

graft_eps = 1e-06
rows = 8


def swap_core(value):
    return lax.ppermute(value, "core", [(0, 1), (1, 0)])


def place_kernel(order, partial, sent_out, kept_out):
    core = lax.axis_index("core")
    group_size = order.shape[0] // 8
    for chip in range(4):
        for i in range(group_size):
            place = chip * group_size + i
            sent_out[place] = partial[order[(2 * chip + 1 - core) * group_size + i]]
            kept_out[place] = partial[order[(2 * chip + core) * group_size + i]]


def place(order, partial):
    smem = pl.BlockSpec(memory_space=pltpu.SMEM)
    vmem = pl.BlockSpec(memory_space=pltpu.VMEM)
    half = jax.ShapeDtypeStruct((partial.shape[0] // 2,) + partial.shape[1:], partial.dtype)
    return pl.pallas_call(
        place_kernel,
        out_shape=(half, half),
        in_specs=[smem, vmem],
        out_specs=(vmem, vmem),
        compiler_params=pltpu.CompilerParams(vmem_limit_bytes=32 * 1024 * 1024),
        cost_estimate=pl.CostEstimate(
            flops=partial.size, bytes_accessed=4 * partial.size, transcendentals=0
        ),
    )(order, partial)


def first_of_group(group_size):
    return lax.axis_index(("x", "core")) * group_size


def slots_kernel(owners, chips, outgoing):
    group_size = chips.shape[1]
    first = first_of_group(group_size)
    outgoing[...] = jnp.zeros_like(outgoing)
    for i in range(group_size):
        total = chips[0, i].astype(jnp.float32)
        for x in range(1, chips.shape[0]):
            total += chips[x, i].astype(jnp.float32)
        outgoing[owners[first + i]] = total.astype(jnp.bfloat16)


def slots(owners, chips, shard_count):
    vmem = pl.BlockSpec(memory_space=pltpu.VMEM)
    return pl.pallas_call(
        slots_kernel,
        out_shape=jax.ShapeDtypeStruct((shard_count,) + chips.shape[2:], chips.dtype),
        in_specs=[pl.BlockSpec(memory_space=pltpu.SMEM), vmem],
        out_specs=vmem,
        compiler_params=pltpu.CompilerParams(vmem_limit_bytes=32 * 1024 * 1024),
        cost_estimate=pl.CostEstimate(
            flops=chips.size, bytes_accessed=4 * chips.size, transcendentals=0
        ),
    )(owners, chips)


def middle_kernel(owns, received, left, right, block_out, grafted_out):
    size = left.shape[0]
    plain = jnp.where(owns[0] > 0, received[...], jnp.zeros_like(received))
    block_out[...] = plain
    block = plain.astype(jnp.float32)
    half = jnp.dot(left[...], plain, preferred_element_type=jnp.float32).astype(jnp.bfloat16)
    shaped = jnp.dot(half, right[...], preferred_element_type=jnp.float32)
    scale = 1.0 / (size * size)
    ratio = jnp.sqrt(jnp.sum(block * block, keepdims=True) * scale + graft_eps) / jnp.sqrt(
        jnp.sum(shaped * shaped, keepdims=True) * scale + graft_eps
    )
    grafted_out[...] = (shaped * ratio).astype(jnp.bfloat16)


def middle(owns, received, left, right):
    size = left.shape[0]
    vmem = pl.BlockSpec(memory_space=pltpu.VMEM)
    return pl.pallas_call(
        middle_kernel,
        out_shape=(jax.ShapeDtypeStruct((size, size), jnp.bfloat16),) * 2,
        in_specs=[pl.BlockSpec(memory_space=pltpu.SMEM)] + [vmem] * 3,
        out_specs=(vmem, vmem),
        compiler_params=pltpu.CompilerParams(vmem_limit_bytes=32 * 1024 * 1024),
        cost_estimate=pl.CostEstimate(
            flops=4 * size * size * size, bytes_accessed=10 * size * size, transcendentals=2
        ),
    )(owns, received, left, right)


def per_device(grad_partial, block_order, owner_slot, left_root, right_root):
    shard_count = lax.axis_size("z") * lax.axis_size("y")
    block_size = left_root.shape[2]
    group_size = grad_partial.shape[1] // (2 * lax.axis_size("x"))

    partial = grad_partial[0].reshape(-1, rows, block_size)
    sent, kept = place(block_order, partial)
    owners = lax.dynamic_slice_in_dim(owner_slot, first_of_group(group_size), group_size)
    owns = jnp.any(owners == lax.axis_index(("z", "y"))).astype(jnp.int32)[None]
    kept, owns = lax.optimization_barrier((kept, owns))
    chip = kept + swap_core(sent)
    chips = lax.all_to_all(chip, "x", 0, 0, tiled=True)
    outgoing = slots(owner_slot, chips.reshape(-1, group_size, rows, block_size), shard_count)
    received = lax.all_to_all(outgoing, ("z", "y"), 0, 0, tiled=True)
    block, grafted = middle(
        owns, received.reshape(block_size, block_size), left_root[0, 0], right_root[0, 0]
    )
    returned = lax.all_to_all(
        grafted.reshape(shard_count, rows, block_size), ("z", "y"), 0, 0, tiled=True
    )
    update = jnp.take(returned, owners, axis=0, mode="clip").reshape(group_size, -1)
    left_stat = jnp.einsum("ab,cb->ac", block, block, preferred_element_type=jnp.float32)
    right_stat = jnp.einsum("ba,bc->ac", block, block, preferred_element_type=jnp.float32)
    return (left_stat[None, None] / block_size, right_stat[None, None] / block_size, update)


def solution(mesh):
    rep_count, shard_count = mesh.devices.shape
    split = Mesh(
        mesh.devices.reshape(rep_count // 2, 2, shard_count // 4, 4), ("x", "core", "z", "y")
    )
    return jax.shard_map(
        per_device,
        mesh=split,
        in_specs=(
            P(("x", "core"), None, ("z", "y")),
            P(),
            P(),
            P(("x", "core"), ("z", "y"), None, None),
            P(("x", "core"), ("z", "y"), None, None),
        ),
        out_specs=(
            P(("x", "core"), ("z", "y"), None, None),
            P(("x", "core"), ("z", "y"), None, None),
            P(("x", "core"), ("z", "y")),
        ),
        check_vma=False,
    )
```

time: 119 us -> 117 us (0.983)
  blocking collectives: 0 us -> 66.8 us
  waiting for transfers between devices: 73.7 us -> 29.9 us
  starting transfers between devices: 30.9 us -> 7.87 us
    all_to_all x0 -> x2, blocking collectives: none -> 66.8 us  [the longest x1 50.1 us: per_device(): received = lax.all_to_all(outgoing, ('z', 'y'), 0, 0, tiled=True)]
    all_to_all x2 -> x0, waiting for transfers between devices: 42.4 us -> none  [the longest x1 30.6 us: per_device(): received = lax.all_to_all(outgoing, ('z', 'y'), 0, 0, tiled=True)]
    all_to_all x2 -> x0, starting transfers between devices: 23 us -> none  [the longest x1 18.7 us: per_device(): received = lax.all_to_all(outgoing, ('z', 'y'), 0, 0, tiled=True)]
    ppermute x1, waiting for transfers between devices: 2.25 us -> 0.87 us  [swap_core(): return lax.ppermute(value, 'core', [(0, 1), (1, 0)])]
  transfers between devices with their start and end apart: 4 -> 2, of which waited for: 4 -> 2; matrix products, arithmetic and copies ran while one was open for 4% -> 3% of each run, Pallas kernels for 0% -> 0%
where the time goes in v3:
time: 117 us; the launch traced here: 116 us
  blocking collectives  66.8 us (57%)
  waiting for transfers between devices  29.9 us (26%)
  starting transfers between devices  7.87 us (7%)
  local copies, waits for them, and re-layouts  3.38 us (3%)
  Pallas kernels  3.34 us (3%)
  matrix products  2.89 us (2%)
  between operations  1.38 us (1%)
    all_to_all x1, blocking collectives, per_device(): received = lax.all_to_all(outgoing, ('z', 'y'), 0, 0, tiled=True)  50.1 us
    all_to_all x1, waiting for transfers between devices, per_device(): lax.all_to_all(grafted.reshape(shard_count, rows, block_size), ('z', 'y')...  29 us
    all_to_all x1, blocking collectives, per_device(): chips = lax.all_to_all(chip, 'x', 0, 0, tiled=True)  16.7 us
    all_to_all x1, starting transfers between devices, per_device(): lax.all_to_all(grafted.reshape(shard_count, rows, block_size), ('z', 'y')...  5.95 us
    unnamed x10, local copies, waits for them, and re-layouts  2.81 us
  transfers between devices with their start and end apart: 2, of which 2 were waited for; matrix products, arithmetic and copies ran while one was open for 3% of the time, Pallas kernels for 0%

profile of v3, /device:TPU:8, one launch (start us, length us, event | category | flops | bytes accessed | tf_op | source)
XLA Modules:
  0.0 116.5 jit_solution(131409797157911382)
XLA Ops:
  0.6 0.0 copy-start.1
  0.6 2.1 %copy.8 = bf16[24,8,8,512]{3,2,1,0:T(8,128)(2,1)S(1)} copy(bf16[24,8,8,512]{3,1,2,0:T(8,128)(2,1)} %bitcast.24) | data formatting | bytes 3145728
  2.7 0.0 copy-start
  2.7 0.0 copy-done.1
  2.7 0.8 shard_map.76
  3.5 1.9 %collective-permute-start = (bf16[96,8,512]{2,1,0:T(8,128)(2,1)S(1)}, bf16[96,8,512]{2,1,0:T(8,128)(2,1)S(1)}, u32[]{:S(2)}, u32[]{:S(2)}) collective-permute-start(bf16[96,8,512]{2,1,0:T(8,128)(2,1)S(1)} %get-tuple-element.12), channel_id=1, source_target_pairs={{0,64},{64,0},{1,65},{65,1},{2,66},{66,2},{3,67},{67,3},{4,68},{68... | collective-permute-start | bytes 2359304 | tf_op jit(solution)/shard_map/ppermute | solution.py:13
  5.4 0.0 copy-done
  5.4 0.7 compare_reduce_fusion
  6.8 0.9 collective-permute-done
  7.7 0.2 add.15
  7.9 16.7 %all_to_all.15 = bf16[96,8,512]{2,1,0:T(8,128)(2,1)S(1)} all-to-all(bf16[96,8,512]{2,1,0:T(8,128)(2,1)S(1)} %add.15), channel_id=1, replica_groups=mesh['x'=4,'core'=2,'z'=16,'y'=4] {'x'}, dimensions={0} | all-to-all | bytes 1572864 | tf_op jit(solution)/shard_map/all_to_all | solution.py:111
  24.6 0.0 copy-start.2
  24.6 0.0 copy-start.3
  24.6 0.7 shard_map.77
  25.3 50.1 %all_to_all.16 = bf16[64,8,512]{2,1,0:T(8,128)(2,1)S(1)} all-to-all(bf16[64,8,512]{2,1,0:T(8,128)(2,1)S(1)} %shard_map.77), channel_id=1, replica_groups=mesh['x'=4,'core'=2,'z'=16,'y'=4] {'z','y'}, dimensions={0} | all-to-all | bytes 1048576 | tf_op jit(solution)/shard_map/all_to_all | solution.py:113
  75.3 0.0 copy-done.2
  75.3 0.0 copy-done.3
  75.3 1.9 %shard_map.78 = (bf16[512,512]{1,0:T(8,128)(2,1)S(1)}, bf16[512,512]{1,0:T(8,128)(2,1)}) custom-call(s32[1]{0:T(128)} %bitcast.owns, bf16[512,512]{1,0:T(8,128)(2,1)S(1)} %bitcast.21, bf16[512,512]{1,0:T(8,128)(2,1)S(1)} %bitcast.22, bf16[512,512]{1,0:T(8,128)(2,1)S(1)} %bitcast.23), custom_call_target="tpu_custom_call" | custom-call | flops 536870912 | bytes 2621440 | tf_op jit(solution)/shard_map/pallas_call | solution.py:88
  77.3 6.0 %all-to-all-start.2 = ((bf16[64,8,512]{2,1,0:T(8,128)(2,1)}), bf16[64,8,512]{2,1,0:T(8,128)(2,1)S(1)}, u32[]{:S(2)}, u32[]{:S(2)}) async-start(bf16[64,8,512]{2,1,0:T(8,128)(2,1)} %bitcast.7), calls=%async_computation.2 | async-start | bytes 1048576 | tf_op jit(solution)/shard_map/all_to_all | solution.py:117
  83.2 1.4 %fusion.1 = f32[1,1,512,512]{3,2,1,0:T(8,128)} fusion(bf16[512,512]{1,0:T(8,128)(2,1)S(1)} %get-tuple-element.13), kind=kOutput, calls=%fused_computation.4 | convolution fusion | flops 268697600 | bytes 1572864 | tf_op jit(solution)/shard_map/ab,cb->ac/dot_general | solution.py:121
  84.7 1.4 %fusion = f32[1,1,512,512]{3,2,1,0:T(8,128)} fusion(bf16[512,512]{1,0:T(8,128)(2,1)S(1)} %get-tuple-element.13), kind=kOutput, calls=%fused_computation.2 | convolution fusion | flops 268697600 | bytes 1572864 | tf_op jit(solution)/shard_map/ba,bc->ac/dot_general | solution.py:122
  86.1 29.0 %all-to-all-done.2 = bf16[64,8,512]{2,1,0:T(8,128)(2,1)S(1)} async-done(((bf16[64,8,512]{2,1,0:T(8,128)(2,1)}), bf16[64,8,512]{2,1,0:T(8,128)(2,1)S(1)}, u32[]{:S(2)}, u32[]{:S(2)}) %all-to-all-start.2) | async-done | bytes 524320 | tf_op jit(solution)/shard_map/all_to_all | solution.py:117
  115.2 0.6 gather_fusion
  115.7 0.7 copy.9
  (1 shorter events, 0.0 us)
Async XLA Ops:
  0.6 2.1 %copy-start.1 = (s32[192]{0:T(256)S(1)}, s32[192]{0:T(256)}, u32[]{:S(2)}) copy-start(s32[192]{0:T(256)} %order.1) | copy-start | bytes 2308
  2.7 2.7 %copy-start = (s32[192]{0:T(256)S(1)}, s32[192]{0:T(256)}, u32[]{:S(2)}) copy-start(s32[192]{0:T(256)} %owners.1) | copy-start | bytes 2308
  3.5 4.2 %collective-permute-start = (bf16[96,8,512]{2,1,0:T(8,128)(2,1)S(1)}, bf16[96,8,512]{2,1,0:T(8,128)(2,1)S(1)}, u32[]{:S(2)}, u32[]{:S(2)}) collective-permute-start(bf16[96,8,512]{2,1,0:T(8,128)(2,1)S(1)} %get-tuple-element.12), channel_id=1, source_target_pairs={{0,64},{64,0},{1,65},{65,1},{2,66},{66,2},{3,67},{67,3},{4,68},{68... | collective-permute-start | bytes 2359304 | tf_op jit(solution)/shard_map/ppermute | solution.py:13
  24.6 50.8 %copy-start.2 = (bf16[1,1,512,512]{3,2,1,0:T(8,128)(2,1)S(1)}, bf16[1,1,512,512]{3,2,1,0:T(8,128)(2,1)}, u32[]{:S(2)}) copy-start(bf16[1,1,512,512]{3,2,1,0:T(8,128)(2,1)} %param.8) | copy-start | bytes 1572868
  24.6 50.8 %copy-start.3 = (bf16[1,1,512,512]{3,2,1,0:T(8,128)(2,1)S(1)}, bf16[1,1,512,512]{3,2,1,0:T(8,128)(2,1)}, u32[]{:S(2)}) copy-start(bf16[1,1,512,512]{3,2,1,0:T(8,128)(2,1)} %param.9) | copy-start | bytes 1572868
  77.3 37.9 %all-to-all-start.2 = ((bf16[64,8,512]{2,1,0:T(8,128)(2,1)}), bf16[64,8,512]{2,1,0:T(8,128)(2,1)S(1)}, u32[]{:S(2)}, u32[]{:S(2)}) async-start(bf16[64,8,512]{2,1,0:T(8,128)(2,1)} %bitcast.7), calls=%async_computation.2 | async-start | bytes 1048576 | tf_op jit(solution)/shard_map/all_to_all | solution.py:117

commit v4 on v3

--- a/solution.py
+++ b/solution.py
@@ -43,29 +43,34 @@
     return lax.axis_index(("x", "core")) * group_size
 
 
-def slots_kernel(owners, chips, outgoing):
-    group_size = chips.shape[1]
+def slots_kernel(owners, *refs):
+    parts, outgoing = refs[:-1], refs[-1]
+    group_size = parts[0].shape[1]
     first = first_of_group(group_size)
     outgoing[...] = jnp.zeros_like(outgoing)
     for i in range(group_size):
-        total = chips[0, i].astype(jnp.float32)
-        for x in range(1, chips.shape[0]):
-            total += chips[x, i].astype(jnp.float32)
-        outgoing[owners[first + i]] = total.astype(jnp.bfloat16)
+        begin = 0
+        for chips in parts:
+            end = begin + chips.shape[3]
+            total = chips[0, i].astype(jnp.float32)
+            for x in range(1, chips.shape[0]):
+                total += chips[x, i].astype(jnp.float32)
+            outgoing[owners[first + i], :, begin:end] = total.astype(jnp.bfloat16)
+            begin = end
 
 
-def slots(owners, chips, shard_count):
+def slots(owners, parts, shard_count):
     vmem = pl.BlockSpec(memory_space=pltpu.VMEM)
+    size = sum(chips.size for chips in parts)
+    width = sum(chips.shape[3] for chips in parts)
     return pl.pallas_call(
         slots_kernel,
-        out_shape=jax.ShapeDtypeStruct((shard_count,) + chips.shape[2:], chips.dtype),
-        in_specs=[pl.BlockSpec(memory_space=pltpu.SMEM), vmem],
+        out_shape=jax.ShapeDtypeStruct((shard_count, rows, width), jnp.bfloat16),
+        in_specs=[pl.BlockSpec(memory_space=pltpu.SMEM)] + [vmem] * len(parts),
         out_specs=vmem,
         compiler_params=pltpu.CompilerParams(vmem_limit_bytes=32 * 1024 * 1024),
-        cost_estimate=pl.CostEstimate(
-            flops=chips.size, bytes_accessed=4 * chips.size, transcendentals=0
-        ),
-    )(owners, chips)
+        cost_estimate=pl.CostEstimate(flops=size, bytes_accessed=4 * size, transcendentals=0),
+    )(owners, *parts)
 
 
 def middle_kernel(owns, received, left, right, block_out, grafted_out):
@@ -108,8 +113,21 @@
     owns = jnp.any(owners == lax.axis_index(("z", "y"))).astype(jnp.int32)[None]
     kept, owns = lax.optimization_barrier((kept, owns))
     chip = kept + swap_core(sent)
-    chips = lax.all_to_all(chip, "x", 0, 0, tiled=True)
-    outgoing = slots(owner_slot, chips.reshape(-1, group_size, rows, block_size), shard_count)
+
+    def chip_sums(shares):
+        def exchange(chip):
+            parts, begin = [], 0
+            for share in shares:
+                end = begin + share * block_size // sum(shares)
+                part = lax.all_to_all(chip[:, :, begin:end], "x", 0, 0, tiled=True)
+                parts.append(part.reshape(-1, group_size, rows, end - begin))
+                begin = end
+            return slots(owner_slot, parts, shard_count)
+
+        return exchange
+
+    at_once, in_turn = chip_sums((1,)), chip_sums((1, 3))
+    outgoing = lax.cond(lax.axis_index("core") == 1, at_once, in_turn, chip)
     received = lax.all_to_all(outgoing, ("z", "y"), 0, 0, tiled=True)
     block, grafted = middle(
         owns, received.reshape(block_size, block_size), left_root[0, 0], right_root[0, 0]

time: 117 us -> 106 us (0.906)
  blocking collectives: 66.8 us -> 52.4 us
  starting transfers between devices: 7.87 us -> 12.2 us
  waiting for transfers between devices: 29.9 us -> 28.2 us
    all_to_all x1, waiting for transfers between devices: 29 us -> 20 us  [per_device(): lax.all_to_all(grafted.reshape(shard_count, rows, block_size), ('z', 'y')...]
    all_to_all x1, blocking collectives: 50.1 us -> 41.6 us  [per_device(): received = lax.all_to_all(outgoing, ('z', 'y'), 0, 0, tiled=True)]
    all_to_all x0 -> x1, waiting for transfers between devices: none -> 7.39 us  [exchange(): part = lax.all_to_all(chip[:, :, begin:end], 'x', 0, 0, tiled=True)]
    all_to_all x1, blocking collectives: 16.7 us -> 10.8 us  [exchange(): part = lax.all_to_all(chip[:, :, begin:end], 'x', 0, 0, tiled=True)]
    all_to_all x0 -> x1, starting transfers between devices: none -> 4.29 us  [exchange(): part = lax.all_to_all(chip[:, :, begin:end], 'x', 0, 0, tiled=True)]
  transfers between devices with their start and end apart: 2 -> 3, of which waited for: 2 -> 3; matrix products, arithmetic and copies ran while one was open for 3% -> 3% of each run, Pallas kernels for 0% -> 0%
where the time goes in v4:
time: 106 us
  blocking collectives  52.4 us (49%)
  waiting for transfers between devices  28.2 us (27%)
  starting transfers between devices  12.2 us (12%)
  local copies, waits for them, and re-layouts  4.14 us (4%)
  Pallas kernels  3.36 us (3%)
  matrix products  2.89 us (3%)
  between operations  1.4 us (1%)
    all_to_all x1, blocking collectives, per_device(): received = lax.all_to_all(outgoing, ('z', 'y'), 0, 0, tiled=True)  41.6 us
    all_to_all x1, waiting for transfers between devices, per_device(): lax.all_to_all(grafted.reshape(shard_count, rows, block_size), ('z', 'y')...  20 us
    all_to_all x1, blocking collectives, exchange(): part = lax.all_to_all(chip[:, :, begin:end], 'x', 0, 0, tiled=True)  10.8 us
    all_to_all x1, waiting for transfers between devices, exchange(): part = lax.all_to_all(chip[:, :, begin:end], 'x', 0, 0, tiled=True)  7.39 us
    all_to_all x1, starting transfers between devices, per_device(): lax.all_to_all(grafted.reshape(shard_count, rows, block_size), ('z', 'y')...  5.98 us
    all_to_all x1, starting transfers between devices, exchange(): part = lax.all_to_all(chip[:, :, begin:end], 'x', 0, 0, tiled=True)  4.29 us
    unnamed x10, local copies, waits for them, and re-layouts  2.82 us
  transfers between devices with their start and end apart: 3, of which 3 were waited for; matrix products, arithmetic and copies ran while one was open for 3% of the time, Pallas kernels for 0%

profile of v4, /device:TPU:8, one launch (start us, length us, event | category | flops | bytes accessed | tf_op | source)
XLA Modules:
  0.0 105.6 jit_solution(7523230565232200276)
XLA Ops:
  0.6 0.0 copy-start
  0.6 2.1 %copy.8 = bf16[24,8,8,512]{3,2,1,0:T(8,128)(2,1)S(1)} copy(bf16[24,8,8,512]{3,1,2,0:T(8,128)(2,1)} %bitcast.28) | data formatting | bytes 3145728
  2.7 0.0 copy-start.3
  2.7 0.0 copy-done
  2.7 0.8 shard_map.76
  3.5 1.9 %collective-permute-start = (bf16[96,8,512]{2,1,0:T(8,128)(2,1)S(1)}, bf16[96,8,512]{2,1,0:T(8,128)(2,1)S(1)}, u32[]{:S(2)}, u32[]{:S(2)}) collective-permute-start(bf16[96,8,512]{2,1,0:T(8,128)(2,1)S(1)} %get-tuple-element.27), channel_id=1, source_target_pairs={{0,64},{64,0},{1,65},{65,1},{2,66},{66,2},{3,67},{67,3},{4,68},{68... | collective-permute-start | bytes 2359304 | tf_op jit(solution)/shard_map/ppermute | solution.py:13
  5.4 0.0 copy-done.3
  5.4 0.7 compare_reduce_fusion
  6.8 0.9 collective-permute-done
  7.7 0.2 add.15
  7.9 0.0 copy-start.1
  7.9 0.0 copy-start.2
  7.9 23.9 %conditional.1 = (bf16[64,8,512]{2,1,0:T(8,128)(2,1)S(1)}) conditional(s32[]{:T(128)} %convert_element_type.4, (bf16[96,8,512]{2,1,0:T(8,128)(2,1)S(1)}, s32[192]{0:T(256)S(1)}) %tuple.21, (bf16[96,8,512]{2,1,0:T(8,128)(2,1)S(1)}, s32[192]{0:T(256)S(1)}) %tuple.22), branch_computations={%region_1.0_spmd, %region_2.0_spmd} | conditional | flops 393216 | bytes 4915240 | solution.py:130
  7.9 0.7 slice.4
  8.6 4.3 %all-to-all-start = ((bf16[96,8,128]{2,1,0:T(8,128)(2,1)}), bf16[96,8,128]{2,1,0:T(8,128)(2,1)S(1)}, u32[]{:S(2)}, u32[]{:S(2)}) async-start(bf16[96,8,128]{2,1,0:T(8,128)(2,1)} %slice.4), calls=%async_computation | async-start | bytes 393216 | tf_op jit(solution)/shard_map/cond/branch_0_fun/all_to_all | solution.py:122
  12.9 0.1 slice.5
  13.0 7.4 %all-to-all-done = bf16[96,8,128]{2,1,0:T(8,128)(2,1)S(1)} async-done(((bf16[96,8,128]{2,1,0:T(8,128)(2,1)}), bf16[96,8,128]{2,1,0:T(8,128)(2,1)S(1)}, u32[]{:S(2)}, u32[]{:S(2)}) %all-to-all-start) | async-done | bytes 196640 | tf_op jit(solution)/shard_map/cond/branch_0_fun/all_to_all | solution.py:122
  20.4 10.8 %all_to_all.22 = bf16[96,8,384]{2,1,0:T(8,128)(2,1)S(1)} all-to-all(bf16[96,8,384]{2,1,0:T(8,128)(2,1)S(1)} %slice.5), channel_id=1, replica_groups=mesh['x'=4,'core'=2,'z'=16,'y'=4] {'x'}, dimensions={0} | all-to-all | bytes 1179648 | tf_op jit(solution)/shard_map/cond/branch_0_fun/all_to_all | solution.py:122
  31.2 0.7 branch_0_fun.1
  31.9 41.6 %all_to_all.24 = bf16[64,8,512]{2,1,0:T(8,128)(2,1)S(1)} all-to-all(bf16[64,8,512]{2,1,0:T(8,128)(2,1)S(1)} %get-tuple-element.32), channel_id=1, replica_groups=mesh['x'=4,'core'=2,'z'=16,'y'=4] {'z','y'}, dimensions={0} | all-to-all | bytes 1048576 | tf_op jit(solution)/shard_map/all_to_all | solution.py:131
  73.5 0.0 copy-done.1
  73.5 0.0 copy-done.2
  73.5 1.9 %shard_map.77 = (bf16[512,512]{1,0:T(8,128)(2,1)S(1)}, bf16[512,512]{1,0:T(8,128)(2,1)}) custom-call(s32[1]{0:T(128)} %bitcast.3.owns, bf16[512,512]{1,0:T(8,128)(2,1)S(1)} %bitcast.25, bf16[512,512]{1,0:T(8,128)(2,1)S(1)} %bitcast.26, bf16[512,512]{1,0:T(8,128)(2,1)S(1)} %bitcast.27), custom_call_target="tpu_custom_call" | custom-call | flops 536870912 | bytes 2621440 | tf_op jit(solution)/shard_map/pallas_call | solution.py:93
  75.4 6.0 %all-to-all-start.4 = ((bf16[64,8,512]{2,1,0:T(8,128)(2,1)}), bf16[64,8,512]{2,1,0:T(8,128)(2,1)S(1)}, u32[]{:S(2)}, u32[]{:S(2)}) async-start(bf16[64,8,512]{2,1,0:T(8,128)(2,1)} %bitcast.9), calls=%async_computation.4 | async-start | bytes 1048576 | tf_op jit(solution)/shard_map/all_to_all | solution.py:135
  81.4 1.4 %fusion.1 = f32[1,1,512,512]{3,2,1,0:T(8,128)} fusion(bf16[512,512]{1,0:T(8,128)(2,1)S(1)} %get-tuple-element.28), kind=kOutput, calls=%fused_computation.4 | convolution fusion | flops 268697600 | bytes 1572864 | tf_op jit(solution)/shard_map/ab,cb->ac/dot_general | solution.py:139
  82.9 1.4 %fusion = f32[1,1,512,512]{3,2,1,0:T(8,128)} fusion(bf16[512,512]{1,0:T(8,128)(2,1)S(1)} %get-tuple-element.28), kind=kOutput, calls=%fused_computation.2 | convolution fusion | flops 268697600 | bytes 1572864 | tf_op jit(solution)/shard_map/ba,bc->ac/dot_general | solution.py:140
  84.3 20.0 %all-to-all-done.4 = bf16[64,8,512]{2,1,0:T(8,128)(2,1)S(1)} async-done(((bf16[64,8,512]{2,1,0:T(8,128)(2,1)}), bf16[64,8,512]{2,1,0:T(8,128)(2,1)S(1)}, u32[]{:S(2)}, u32[]{:S(2)}) %all-to-all-start.4) | async-done | bytes 524320 | tf_op jit(solution)/shard_map/all_to_all | solution.py:135
  104.3 0.6 gather_fusion
  104.9 0.7 copy.9
  (1 shorter events, 0.0 us)
Async XLA Ops:
  0.6 2.1 %copy-start = (s32[192]{0:T(256)S(1)}, s32[192]{0:T(256)}, u32[]{:S(2)}) copy-start(s32[192]{0:T(256)} %order.1) | copy-start | bytes 2308
  2.7 2.7 %copy-start.3 = (s32[192]{0:T(256)S(1)}, s32[192]{0:T(256)}, u32[]{:S(2)}) copy-start(s32[192]{0:T(256)} %param.9) | copy-start | bytes 2308
  3.5 4.2 %collective-permute-start = (bf16[96,8,512]{2,1,0:T(8,128)(2,1)S(1)}, bf16[96,8,512]{2,1,0:T(8,128)(2,1)S(1)}, u32[]{:S(2)}, u32[]{:S(2)}) collective-permute-start(bf16[96,8,512]{2,1,0:T(8,128)(2,1)S(1)} %get-tuple-element.27), channel_id=1, source_target_pairs={{0,64},{64,0},{1,65},{65,1},{2,66},{66,2},{3,67},{67,3},{4,68},{68... | collective-permute-start | bytes 2359304 | tf_op jit(solution)/shard_map/ppermute | solution.py:13
  7.9 65.6 %copy-start.1 = (bf16[1,1,512,512]{3,2,1,0:T(8,128)(2,1)S(1)}, bf16[1,1,512,512]{3,2,1,0:T(8,128)(2,1)}, u32[]{:S(2)}) copy-start(bf16[1,1,512,512]{3,2,1,0:T(8,128)(2,1)} %param.10) | copy-start | bytes 1572868
  7.9 65.6 %copy-start.2 = (bf16[1,1,512,512]{3,2,1,0:T(8,128)(2,1)S(1)}, bf16[1,1,512,512]{3,2,1,0:T(8,128)(2,1)}, u32[]{:S(2)}) copy-start(bf16[1,1,512,512]{3,2,1,0:T(8,128)(2,1)} %param.11) | copy-start | bytes 1572868
  8.6 11.7 %all-to-all-start = ((bf16[96,8,128]{2,1,0:T(8,128)(2,1)}), bf16[96,8,128]{2,1,0:T(8,128)(2,1)S(1)}, u32[]{:S(2)}, u32[]{:S(2)}) async-start(bf16[96,8,128]{2,1,0:T(8,128)(2,1)} %slice.4), calls=%async_computation | async-start | bytes 393216 | tf_op jit(solution)/shard_map/cond/branch_0_fun/all_to_all | solution.py:122
  75.4 28.9 %all-to-all-start.4 = ((bf16[64,8,512]{2,1,0:T(8,128)(2,1)}), bf16[64,8,512]{2,1,0:T(8,128)(2,1)S(1)}, u32[]{:S(2)}, u32[]{:S(2)}) async-start(bf16[64,8,512]{2,1,0:T(8,128)(2,1)} %bitcast.9), calls=%async_computation.4 | async-start | bytes 1048576 | tf_op jit(solution)/shard_map/all_to_all | solution.py:135

commit v5 on v4

--- a/solution.py
+++ b/solution.py
@@ -45,27 +45,23 @@
 
 def slots_kernel(owners, *refs):
     parts, outgoing = refs[:-1], refs[-1]
-    group_size = parts[0].shape[1]
-    first = first_of_group(group_size)
+    first = first_of_group(sum(chips.shape[1] for chips in parts))
     outgoing[...] = jnp.zeros_like(outgoing)
-    for i in range(group_size):
-        begin = 0
-        for chips in parts:
-            end = begin + chips.shape[3]
+    for chips in parts:
+        for i in range(chips.shape[1]):
             total = chips[0, i].astype(jnp.float32)
             for x in range(1, chips.shape[0]):
                 total += chips[x, i].astype(jnp.float32)
-            outgoing[owners[first + i], :, begin:end] = total.astype(jnp.bfloat16)
-            begin = end
+            outgoing[owners[first + i]] = total.astype(jnp.bfloat16)
+        first += chips.shape[1]
 
 
 def slots(owners, parts, shard_count):
     vmem = pl.BlockSpec(memory_space=pltpu.VMEM)
     size = sum(chips.size for chips in parts)
-    width = sum(chips.shape[3] for chips in parts)
     return pl.pallas_call(
         slots_kernel,
-        out_shape=jax.ShapeDtypeStruct((shard_count, rows, width), jnp.bfloat16),
+        out_shape=jax.ShapeDtypeStruct((shard_count,) + parts[0].shape[2:], jnp.bfloat16),
         in_specs=[pl.BlockSpec(memory_space=pltpu.SMEM)] + [vmem] * len(parts),
         out_specs=vmem,
         compiler_params=pltpu.CompilerParams(vmem_limit_bytes=32 * 1024 * 1024),
@@ -114,19 +110,19 @@
     kept, owns = lax.optimization_barrier((kept, owns))
     chip = kept + swap_core(sent)
 
-    def chip_sums(shares):
+    def chip_sums(counts):
         def exchange(chip):
+            chip = chip.reshape(-1, group_size, rows, block_size)
             parts, begin = [], 0
-            for share in shares:
-                end = begin + share * block_size // sum(shares)
-                part = lax.all_to_all(chip[:, :, begin:end], "x", 0, 0, tiled=True)
-                parts.append(part.reshape(-1, group_size, rows, end - begin))
-                begin = end
+            for count in counts:
+                part = chip[:, begin : begin + count]
+                parts.append(lax.all_to_all(part, "x", 0, 0, tiled=True))
+                begin += count
             return slots(owner_slot, parts, shard_count)
 
         return exchange
 
-    at_once, in_turn = chip_sums((1,)), chip_sums((1, 3))
+    at_once, in_turn = chip_sums((group_size,)), chip_sums((2, group_size - 2))
     outgoing = lax.cond(lax.axis_index("core") == 1, at_once, in_turn, chip)
     received = lax.all_to_all(outgoing, ("z", "y"), 0, 0, tiled=True)
     block, grafted = middle(

time: 106 us -> 105 us (level)
  waiting for transfers between devices: 28.2 us -> 26.8 us
    all_to_all x1, waiting for transfers between devices: 7.39 us -> 5.98 us  [exchange(): parts.append(lax.all_to_all(part, 'x', 0, 0, tiled=True))]
where the time goes in v5:
time: 105 us
  blocking collectives  53.2 us (51%)
  waiting for transfers between devices  26.8 us (26%)
  starting transfers between devices  12.2 us (12%)
  local copies, waits for them, and re-layouts  4.07 us (4%)
  Pallas kernels  3.36 us (3%)
  matrix products  2.89 us (3%)
  between operations  1.4 us (1%)
    all_to_all x1, blocking collectives, per_device(): received = lax.all_to_all(outgoing, ('z', 'y'), 0, 0, tiled=True)  41.7 us
    all_to_all x1, waiting for transfers between devices, per_device(): lax.all_to_all(grafted.reshape(shard_count, rows, block_size), ('z', 'y')...  20 us
    all_to_all x1, blocking collectives, exchange(): parts.append(lax.all_to_all(part, 'x', 0, 0, tiled=True))  11.5 us
    all_to_all x1, waiting for transfers between devices, exchange(): parts.append(lax.all_to_all(part, 'x', 0, 0, tiled=True))  5.98 us
    all_to_all x1, starting transfers between devices, per_device(): lax.all_to_all(grafted.reshape(shard_count, rows, block_size), ('z', 'y')...  5.95 us
    all_to_all x1, starting transfers between devices, exchange(): parts.append(lax.all_to_all(part, 'x', 0, 0, tiled=True))  4.29 us
    unnamed x10, local copies, waits for them, and re-layouts  2.82 us
  transfers between devices with their start and end apart: 3, of which 3 were waited for; matrix products, arithmetic and copies ran while one was open for 3% of the time, Pallas kernels for 0%

profile of v5, /device:TPU:8, one launch (start us, length us, event | category | flops | bytes accessed | tf_op | source)
XLA Modules:
  0.0 104.9 jit_solution(5303732123073902055)
XLA Ops:
  0.6 0.0 copy-start
  0.6 2.1 %copy.8 = bf16[24,8,8,512]{3,2,1,0:T(8,128)(2,1)S(1)} copy(bf16[24,8,8,512]{3,1,2,0:T(8,128)(2,1)} %bitcast.27) | data formatting | bytes 3145728
  2.7 0.0 copy-start.3
  2.7 0.0 copy-done
  2.7 0.8 shard_map.76
  3.5 1.9 %collective-permute-start = (bf16[96,8,512]{2,1,0:T(8,128)(2,1)S(1)}, bf16[96,8,512]{2,1,0:T(8,128)(2,1)S(1)}, u32[]{:S(2)}, u32[]{:S(2)}) collective-permute-start(bf16[96,8,512]{2,1,0:T(8,128)(2,1)S(1)} %get-tuple-element.27), channel_id=1, source_target_pairs={{0,64},{64,0},{1,65},{65,1},{2,66},{66,2},{3,67},{67,3},{4,68},{68... | collective-permute-start | bytes 2359304 | tf_op jit(solution)/shard_map/ppermute | solution.py:13
  5.4 0.0 copy-done.3
  5.4 0.7 compare_reduce_fusion
  6.8 0.9 collective-permute-done
  7.7 0.2 add.15
  7.9 0.0 copy-start.1
  7.9 0.0 copy-start.2
  7.9 23.2 %conditional.1 = (bf16[64,8,512]{2,1,0:T(8,128)(2,1)S(1)}) conditional(s32[]{:T(128)} %convert_element_type.4, (bf16[96,8,512]{2,1,0:T(8,128)(2,1)S(1)}, s32[192]{0:T(256)S(1)}) %tuple.21, (bf16[96,8,512]{2,1,0:T(8,128)(2,1)S(1)}, s32[192]{0:T(256)S(1)}) %tuple.22), branch_computations={%region_1.0_spmd, %region_2.0_spmd} | conditional | flops 393216 | bytes 4784168 | solution.py:126
  7.9 0.6 slice.8
  8.6 4.3 %all-to-all-start = ((bf16[4,2,8,512]{3,2,1,0:T(8,128)(2,1)}), bf16[4,2,8,512]{3,2,1,0:T(8,128)(2,1)S(1)}, u32[]{:S(2)}, u32[]{:S(2)}) async-start(bf16[4,2,8,512]{3,2,1,0:T(8,128)(2,1)} %slice.8), calls=%async_computation | async-start | bytes 131072 | tf_op jit(solution)/shard_map/cond/branch_0_fun/all_to_all | solution.py:119
  12.9 0.1 slice.9
  12.9 6.0 %all-to-all-done.refs_0_ = bf16[4,2,8,512]{3,2,1,0:T(8,128)(2,1)S(1)} async-done(((bf16[4,2,8,512]{3,2,1,0:T(8,128)(2,1)}), bf16[4,2,8,512]{3,2,1,0:T(8,128)(2,1)S(1)}, u32[]{:S(2)}, u32[]{:S(2)}) %all-to-all-start) | async-done | bytes 65568 | tf_op jit(solution)/shard_map/cond/branch_0_fun/all_to_all | solution.py:119
  18.9 11.5 %all_to_all.22.refs_1_ = bf16[4,22,8,512]{3,2,1,0:T(8,128)(2,1)S(1)} all-to-all(bf16[4,22,8,512]{3,2,1,0:T(8,128)(2,1)S(1)} %slice.9), channel_id=1, replica_groups=mesh['x'=4,'core'=2,'z'=16,'y'=4] {'x'}, dimensions={0} | all-to-all | bytes 1441792 | tf_op jit(solution)/shard_map/cond/branch_0_fun/all_to_all | solution.py:119
  30.4 0.7 branch_0_fun.1
  31.1 41.7 %all_to_all.24 = bf16[64,8,512]{2,1,0:T(8,128)(2,1)S(1)} all-to-all(bf16[64,8,512]{2,1,0:T(8,128)(2,1)S(1)} %get-tuple-element.32), channel_id=1, replica_groups=mesh['x'=4,'core'=2,'z'=16,'y'=4] {'z','y'}, dimensions={0} | all-to-all | bytes 1048576 | tf_op jit(solution)/shard_map/all_to_all | solution.py:127
  72.8 0.0 copy-done.1
  72.8 0.0 copy-done.2
  72.8 1.9 %shard_map.77 = (bf16[512,512]{1,0:T(8,128)(2,1)S(1)}, bf16[512,512]{1,0:T(8,128)(2,1)}) custom-call(s32[1]{0:T(128)} %bitcast.2.owns, bf16[512,512]{1,0:T(8,128)(2,1)S(1)} %bitcast.21, bf16[512,512]{1,0:T(8,128)(2,1)S(1)} %bitcast.22, bf16[512,512]{1,0:T(8,128)(2,1)S(1)} %bitcast.23), custom_call_target="tpu_custom_call" | custom-call | flops 536870912 | bytes 2621440 | tf_op jit(solution)/shard_map/pallas_call | solution.py:89
  74.7 5.9 %all-to-all-start.4 = ((bf16[64,8,512]{2,1,0:T(8,128)(2,1)}), bf16[64,8,512]{2,1,0:T(8,128)(2,1)S(1)}, u32[]{:S(2)}, u32[]{:S(2)}) async-start(bf16[64,8,512]{2,1,0:T(8,128)(2,1)} %bitcast.8), calls=%async_computation.4 | async-start | bytes 1048576 | tf_op jit(solution)/shard_map/all_to_all | solution.py:131
  80.7 1.4 %fusion.1 = f32[1,1,512,512]{3,2,1,0:T(8,128)} fusion(bf16[512,512]{1,0:T(8,128)(2,1)S(1)} %get-tuple-element.28), kind=kOutput, calls=%fused_computation.4 | convolution fusion | flops 268697600 | bytes 1572864 | tf_op jit(solution)/shard_map/ab,cb->ac/dot_general | solution.py:135
  82.1 1.4 %fusion = f32[1,1,512,512]{3,2,1,0:T(8,128)} fusion(bf16[512,512]{1,0:T(8,128)(2,1)S(1)} %get-tuple-element.28), kind=kOutput, calls=%fused_computation.2 | convolution fusion | flops 268697600 | bytes 1572864 | tf_op jit(solution)/shard_map/ba,bc->ac/dot_general | solution.py:136
  83.6 20.0 %all-to-all-done.4 = bf16[64,8,512]{2,1,0:T(8,128)(2,1)S(1)} async-done(((bf16[64,8,512]{2,1,0:T(8,128)(2,1)}), bf16[64,8,512]{2,1,0:T(8,128)(2,1)S(1)}, u32[]{:S(2)}, u32[]{:S(2)}) %all-to-all-start.4) | async-done | bytes 524320 | tf_op jit(solution)/shard_map/all_to_all | solution.py:131
  103.6 0.6 gather_fusion
  104.1 0.7 copy.9
  (1 shorter events, 0.0 us)
Async XLA Ops:
  0.6 2.1 %copy-start = (s32[192]{0:T(256)S(1)}, s32[192]{0:T(256)}, u32[]{:S(2)}) copy-start(s32[192]{0:T(256)} %order.1) | copy-start | bytes 2308
  2.7 2.7 %copy-start.3 = (s32[192]{0:T(256)S(1)}, s32[192]{0:T(256)}, u32[]{:S(2)}) copy-start(s32[192]{0:T(256)} %param.9) | copy-start | bytes 2308
  3.5 4.2 %collective-permute-start = (bf16[96,8,512]{2,1,0:T(8,128)(2,1)S(1)}, bf16[96,8,512]{2,1,0:T(8,128)(2,1)S(1)}, u32[]{:S(2)}, u32[]{:S(2)}) collective-permute-start(bf16[96,8,512]{2,1,0:T(8,128)(2,1)S(1)} %get-tuple-element.27), channel_id=1, source_target_pairs={{0,64},{64,0},{1,65},{65,1},{2,66},{66,2},{3,67},{67,3},{4,68},{68... | collective-permute-start | bytes 2359304 | tf_op jit(solution)/shard_map/ppermute | solution.py:13
  7.9 64.9 %copy-start.1 = (bf16[1,1,512,512]{3,2,1,0:T(8,128)(2,1)S(1)}, bf16[1,1,512,512]{3,2,1,0:T(8,128)(2,1)}, u32[]{:S(2)}) copy-start(bf16[1,1,512,512]{3,2,1,0:T(8,128)(2,1)} %param.10) | copy-start | bytes 1572868
  7.9 64.9 %copy-start.2 = (bf16[1,1,512,512]{3,2,1,0:T(8,128)(2,1)S(1)}, bf16[1,1,512,512]{3,2,1,0:T(8,128)(2,1)}, u32[]{:S(2)}) copy-start(bf16[1,1,512,512]{3,2,1,0:T(8,128)(2,1)} %param.11) | copy-start | bytes 1572868
  8.6 10.3 %all-to-all-start = ((bf16[4,2,8,512]{3,2,1,0:T(8,128)(2,1)}), bf16[4,2,8,512]{3,2,1,0:T(8,128)(2,1)S(1)}, u32[]{:S(2)}, u32[]{:S(2)}) async-start(bf16[4,2,8,512]{3,2,1,0:T(8,128)(2,1)} %slice.8), calls=%async_computation | async-start | bytes 131072 | tf_op jit(solution)/shard_map/cond/branch_0_fun/all_to_all | solution.py:119
  74.7 28.8 %all-to-all-start.4 = ((bf16[64,8,512]{2,1,0:T(8,128)(2,1)}), bf16[64,8,512]{2,1,0:T(8,128)(2,1)S(1)}, u32[]{:S(2)}, u32[]{:S(2)}) async-start(bf16[64,8,512]{2,1,0:T(8,128)(2,1)} %bitcast.8), calls=%async_computation.4 | async-start | bytes 1048576 | tf_op jit(solution)/shard_map/all_to_all | solution.py:131

commit v6 on v5

--- a/solution.py
+++ b/solution.py
@@ -80,7 +80,12 @@
     ratio = jnp.sqrt(jnp.sum(block * block, keepdims=True) * scale + graft_eps) / jnp.sqrt(
         jnp.sum(shaped * shaped, keepdims=True) * scale + graft_eps
     )
-    grafted_out[...] = (shaped * ratio).astype(jnp.bfloat16)
+    grafted = shaped * ratio
+    z_count = grafted_out.shape[0] // 4
+    for z in range(z_count):
+        for y in range(4):
+            begin = (z * 4 + y) * rows
+            grafted_out[y * z_count + z] = grafted[begin : begin + rows].astype(jnp.bfloat16)
 
 
 def middle(owns, received, left, right):
@@ -88,7 +93,10 @@
     vmem = pl.BlockSpec(memory_space=pltpu.VMEM)
     return pl.pallas_call(
         middle_kernel,
-        out_shape=(jax.ShapeDtypeStruct((size, size), jnp.bfloat16),) * 2,
+        out_shape=(
+            jax.ShapeDtypeStruct((size, size), jnp.bfloat16),
+            jax.ShapeDtypeStruct((size // rows, rows, size), jnp.bfloat16),
+        ),
         in_specs=[pl.BlockSpec(memory_space=pltpu.SMEM)] + [vmem] * 3,
         out_specs=(vmem, vmem),
         compiler_params=pltpu.CompilerParams(vmem_limit_bytes=32 * 1024 * 1024),
@@ -128,10 +136,9 @@
     block, grafted = middle(
         owns, received.reshape(block_size, block_size), left_root[0, 0], right_root[0, 0]
     )
-    returned = lax.all_to_all(
-        grafted.reshape(shard_count, rows, block_size), ("z", "y"), 0, 0, tiled=True
-    )
-    update = jnp.take(returned, owners, axis=0, mode="clip").reshape(group_size, -1)
+    returned = lax.all_to_all(grafted, ("y", "z"), 0, 0, tiled=True)
+    places = owners % 4 * (shard_count // 4) + owners // 4
+    update = jnp.take(returned, places, axis=0, mode="clip").reshape(group_size, -1)
     left_stat = jnp.einsum("ab,cb->ac", block, block, preferred_element_type=jnp.float32)
     right_stat = jnp.einsum("ba,bc->ac", block, block, preferred_element_type=jnp.float32)
     return (left_stat[None, None] / block_size, right_stat[None, None] / block_size, update)

time: 105 us -> 105 us (level)
  transfers between devices with their start and end apart: 3 -> 3, of which waited for: 3 -> 3; matrix products, arithmetic and copies ran while one was open for 3% -> 4% of each run, Pallas kernels for 0% -> 0%
where the time goes in v6:
time: 105 us; the launch traced here: 104 us
  blocking collectives  53.2 us (51%)
  waiting for transfers between devices  26 us (25%)
  starting transfers between devices  12.2 us (12%)
  local copies, waits for them, and re-layouts  4.07 us (4%)
  Pallas kernels  3.35 us (3%)
  matrix products  2.88 us (3%)
  between operations  1.39 us (1%)
    all_to_all x1, blocking collectives, per_device(): received = lax.all_to_all(outgoing, ('z', 'y'), 0, 0, tiled=True)  41.7 us
    all_to_all x1, waiting for transfers between devices, per_device(): returned = lax.all_to_all(grafted, ('y', 'z'), 0, 0, tiled=True)  19.2 us
    all_to_all x1, blocking collectives, exchange(): parts.append(lax.all_to_all(part, 'x', 0, 0, tiled=True))  11.5 us
    all_to_all x1, waiting for transfers between devices, exchange(): parts.append(lax.all_to_all(part, 'x', 0, 0, tiled=True))  5.98 us
    all_to_all x1, starting transfers between devices, per_device(): returned = lax.all_to_all(grafted, ('y', 'z'), 0, 0, tiled=True)  5.96 us
    all_to_all x1, starting transfers between devices, exchange(): parts.append(lax.all_to_all(part, 'x', 0, 0, tiled=True))  4.29 us
    unnamed x10, local copies, waits for them, and re-layouts  2.82 us
  transfers between devices with their start and end apart: 3, of which 3 were waited for; matrix products, arithmetic and copies ran while one was open for 4% of the time, Pallas kernels for 0%

profile of v6, /device:TPU:8, one launch (start us, length us, event | category | flops | bytes accessed | tf_op | source)
XLA Modules:
  0.0 104.1 jit_solution(2627454791125686804)
XLA Ops:
  0.6 0.0 copy-start
  0.6 2.1 %copy.8 = bf16[24,8,8,512]{3,2,1,0:T(8,128)(2,1)S(1)} copy(bf16[24,8,8,512]{3,1,2,0:T(8,128)(2,1)} %bitcast.26) | data formatting | bytes 3145728
  2.7 0.0 copy-start.3
  2.7 0.0 copy-done
  2.7 0.8 shard_map.76
  3.5 1.9 %collective-permute-start = (bf16[96,8,512]{2,1,0:T(8,128)(2,1)S(1)}, bf16[96,8,512]{2,1,0:T(8,128)(2,1)S(1)}, u32[]{:S(2)}, u32[]{:S(2)}) collective-permute-start(bf16[96,8,512]{2,1,0:T(8,128)(2,1)S(1)} %get-tuple-element.27), channel_id=1, source_target_pairs={{0,64},{64,0},{1,65},{65,1},{2,66},{66,2},{3,67},{67,3},{4,68},{68... | collective-permute-start | bytes 2359304 | tf_op jit(solution)/shard_map/ppermute | solution.py:13
  5.4 0.0 copy-done.3
  5.4 0.7 compare_reduce_fusion
  6.8 0.9 collective-permute-done
  7.7 0.2 add.25
  7.9 0.0 copy-start.1
  7.9 0.0 copy-start.2
  7.9 23.2 %conditional.1 = (bf16[64,8,512]{2,1,0:T(8,128)(2,1)S(1)}) conditional(s32[]{:T(128)} %convert_element_type.4, (bf16[96,8,512]{2,1,0:T(8,128)(2,1)S(1)}, s32[192]{0:T(256)S(1)}) %tuple.20, (bf16[96,8,512]{2,1,0:T(8,128)(2,1)S(1)}, s32[192]{0:T(256)S(1)}) %tuple.21), branch_computations={%region_1.0_spmd, %region_2.0_spmd} | conditional | flops 393216 | bytes 4784168 | solution.py:134
  7.9 0.6 slice.8
  8.6 4.3 %all-to-all-start = ((bf16[4,2,8,512]{3,2,1,0:T(8,128)(2,1)}), bf16[4,2,8,512]{3,2,1,0:T(8,128)(2,1)S(1)}, u32[]{:S(2)}, u32[]{:S(2)}) async-start(bf16[4,2,8,512]{3,2,1,0:T(8,128)(2,1)} %slice.8), calls=%async_computation | async-start | bytes 131072 | tf_op jit(solution)/shard_map/cond/branch_0_fun/all_to_all | solution.py:127
  12.9 0.1 slice.9
  12.9 6.0 %all-to-all-done.refs_0_ = bf16[4,2,8,512]{3,2,1,0:T(8,128)(2,1)S(1)} async-done(((bf16[4,2,8,512]{3,2,1,0:T(8,128)(2,1)}), bf16[4,2,8,512]{3,2,1,0:T(8,128)(2,1)S(1)}, u32[]{:S(2)}, u32[]{:S(2)}) %all-to-all-start) | async-done | bytes 65568 | tf_op jit(solution)/shard_map/cond/branch_0_fun/all_to_all | solution.py:127
  18.9 11.5 %all_to_all.22.refs_1_ = bf16[4,22,8,512]{3,2,1,0:T(8,128)(2,1)S(1)} all-to-all(bf16[4,22,8,512]{3,2,1,0:T(8,128)(2,1)S(1)} %slice.9), channel_id=1, replica_groups=mesh['x'=4,'core'=2,'z'=16,'y'=4] {'x'}, dimensions={0} | all-to-all | bytes 1441792 | tf_op jit(solution)/shard_map/cond/branch_0_fun/all_to_all | solution.py:127
  30.4 0.7 branch_0_fun.1
  31.1 41.7 %all_to_all.24 = bf16[64,8,512]{2,1,0:T(8,128)(2,1)S(1)} all-to-all(bf16[64,8,512]{2,1,0:T(8,128)(2,1)S(1)} %get-tuple-element.30), channel_id=1, replica_groups=mesh['x'=4,'core'=2,'z'=16,'y'=4] {'z','y'}, dimensions={0} | all-to-all | bytes 1048576 | tf_op jit(solution)/shard_map/all_to_all | solution.py:135
  72.8 0.0 copy-done.1
  72.8 0.0 copy-done.2
  72.8 1.9 %shard_map.77 = (bf16[512,512]{1,0:T(8,128)(2,1)S(1)}, bf16[64,8,512]{2,1,0:T(8,128)(2,1)}) custom-call(s32[1]{0:T(128)} %bitcast.2.owns, bf16[512,512]{1,0:T(8,128)(2,1)S(1)} %bitcast.20, bf16[512,512]{1,0:T(8,128)(2,1)S(1)} %bitcast.21, bf16[512,512]{1,0:T(8,128)(2,1)S(1)} %bitcast.22), custom_call_target="tpu_custom_call" | custom-call | flops 536870912 | bytes 2621440 | tf_op jit(solution)/shard_map/pallas_call | solution.py:94
  74.7 6.0 %all-to-all-start.4 = ((bf16[64,8,512]{2,1,0:T(8,128)(2,1)}), bf16[64,8,512]{2,1,0:T(8,128)(2,1)S(1)}, u32[]{:S(2)}, u32[]{:S(2)}) async-start(bf16[64,8,512]{2,1,0:T(8,128)(2,1)} %get-tuple-element.29), calls=%async_computation.4 | async-start | bytes 1048576 | tf_op jit(solution)/shard_map/all_to_all | solution.py:139
  80.7 0.1 fusion.3
  80.8 1.4 %fusion.1 = f32[1,1,512,512]{3,2,1,0:T(8,128)} fusion(bf16[512,512]{1,0:T(8,128)(2,1)S(1)} %get-tuple-element.28), kind=kOutput, calls=%fused_computation.4 | convolution fusion | flops 268697600 | bytes 1572864 | tf_op jit(solution)/shard_map/ab,cb->ac/dot_general | solution.py:142
  82.2 1.4 %fusion = f32[1,1,512,512]{3,2,1,0:T(8,128)} fusion(bf16[512,512]{1,0:T(8,128)(2,1)S(1)} %get-tuple-element.28), kind=kOutput, calls=%fused_computation.2 | convolution fusion | flops 268697600 | bytes 1572864 | tf_op jit(solution)/shard_map/ba,bc->ac/dot_general | solution.py:143
  83.6 19.2 %all-to-all-done.4 = bf16[64,8,512]{2,1,0:T(8,128)(2,1)S(1)} async-done(((bf16[64,8,512]{2,1,0:T(8,128)(2,1)}), bf16[64,8,512]{2,1,0:T(8,128)(2,1)S(1)}, u32[]{:S(2)}, u32[]{:S(2)}) %all-to-all-start.4) | async-done | bytes 524320 | tf_op jit(solution)/shard_map/all_to_all | solution.py:139
  102.8 0.6 gather_fusion
  103.4 0.7 copy.9
  (1 shorter events, 0.0 us)
Async XLA Ops:
  0.6 2.1 %copy-start = (s32[192]{0:T(256)S(1)}, s32[192]{0:T(256)}, u32[]{:S(2)}) copy-start(s32[192]{0:T(256)} %order.1) | copy-start | bytes 2308
  2.7 2.7 %copy-start.3 = (s32[192]{0:T(256)S(1)}, s32[192]{0:T(256)}, u32[]{:S(2)}) copy-start(s32[192]{0:T(256)} %param.9) | copy-start | bytes 2308
  3.5 4.2 %collective-permute-start = (bf16[96,8,512]{2,1,0:T(8,128)(2,1)S(1)}, bf16[96,8,512]{2,1,0:T(8,128)(2,1)S(1)}, u32[]{:S(2)}, u32[]{:S(2)}) collective-permute-start(bf16[96,8,512]{2,1,0:T(8,128)(2,1)S(1)} %get-tuple-element.27), channel_id=1, source_target_pairs={{0,64},{64,0},{1,65},{65,1},{2,66},{66,2},{3,67},{67,3},{4,68},{68... | collective-permute-start | bytes 2359304 | tf_op jit(solution)/shard_map/ppermute | solution.py:13
  7.9 64.9 %copy-start.1 = (bf16[1,1,512,512]{3,2,1,0:T(8,128)(2,1)S(1)}, bf16[1,1,512,512]{3,2,1,0:T(8,128)(2,1)}, u32[]{:S(2)}) copy-start(bf16[1,1,512,512]{3,2,1,0:T(8,128)(2,1)} %param.10) | copy-start | bytes 1572868
  7.9 64.9 %copy-start.2 = (bf16[1,1,512,512]{3,2,1,0:T(8,128)(2,1)S(1)}, bf16[1,1,512,512]{3,2,1,0:T(8,128)(2,1)}, u32[]{:S(2)}) copy-start(bf16[1,1,512,512]{3,2,1,0:T(8,128)(2,1)} %param.11) | copy-start | bytes 1572868
  8.6 10.3 %all-to-all-start = ((bf16[4,2,8,512]{3,2,1,0:T(8,128)(2,1)}), bf16[4,2,8,512]{3,2,1,0:T(8,128)(2,1)S(1)}, u32[]{:S(2)}, u32[]{:S(2)}) async-start(bf16[4,2,8,512]{3,2,1,0:T(8,128)(2,1)} %slice.8), calls=%async_computation | async-start | bytes 131072 | tf_op jit(solution)/shard_map/cond/branch_0_fun/all_to_all | solution.py:127
  74.7 28.1 %all-to-all-start.4 = ((bf16[64,8,512]{2,1,0:T(8,128)(2,1)}), bf16[64,8,512]{2,1,0:T(8,128)(2,1)S(1)}, u32[]{:S(2)}, u32[]{:S(2)}) async-start(bf16[64,8,512]{2,1,0:T(8,128)(2,1)} %get-tuple-element.29), calls=%async_computation.4 | async-start | bytes 1048576 | tf_op jit(solution)/shard_map/all_to_all | solution.py:139
